TPU v7x, 32 devices: a whole 2x2x4 slice. The times are simulated.
32 devices in a mesh: dp: 8 (over y, x, core), tensor: 4 (over z).
Axes of the slice: x: 2, y: 2, z: 4, core: 2. Of those that a mesh axis runs over, the one named last changes fastest.
Arguments:
- tokens: bfloat16 [1024, 64, 1024], P('tensor', 'dp'), may hold values from -1.6953125 to 1.6953125
- cond: bfloat16 [64, 1024], P('dp'), may hold values from -1.6953125 to 1.6953125
- cotangent: bfloat16 [1024, 64, 1024], P('tensor', 'dp'), may hold values from -1.6953125 to 1.6953125
- qkv_weight: bfloat16 [1024, 3, 1024], P(None, None, 'tensor'), may hold values from -0.1875 to 0.1875
- qv_bias: bfloat16 [2, 1024], P(None, 'tensor'), may hold values from -0.5 to 0.5
- output_projection_weight: bfloat16 [1024, 1024], P('tensor'), may hold values from -0.75 to 0.75
- proj_bias: bfloat16 [1024], replicated, may hold values from -0.5 to 0.5
- fc1_weight: bfloat16 [1024, 4096], P(None, 'tensor'), may hold values from -0.1875 to 0.1875
- fc1_bias: bfloat16 [4096], P('tensor'), may hold values from -0.5 to 0.5
- fc2_weight: bfloat16 [4096, 1024], P('tensor'), may hold values from -0.09375 to 0.09375
- fc2_bias: bfloat16 [1024], replicated, may hold values from -0.5 to 0.5
- ada_weight: bfloat16 [1024, 6, 1024], P(None, None, 'tensor'), may hold values from -0.1875 to 0.1875
- ada_bias: bfloat16 [6, 1024], P(None, 'tensor'), may hold values from -0.3984375 to 0.3984375
Outputs:
- output: bfloat16 [1024, 64, 1024], P('tensor', 'dp')
- grad_tokens: float32 [1024, 64, 1024], P('tensor', 'dp')
- grad_cond: float32 [64, 1024], P('dp')
- grad_qkv: float32 [1024, 3, 1024], P(None, None, 'tensor')
- grad_qv_bias: float32 [2, 1024], P(None, 'tensor')
- output_projection_gradient: float32 [1024, 1024], P('tensor')
- grad_proj_bias: float32 [1024], replicated
- grad_fc1: float32 [1024, 4096], P(None, 'tensor')
- grad_fc1_bias: float32 [4096], P('tensor')
- grad_fc2: float32 [4096, 1024], P('tensor')
- grad_fc2_bias: float32 [1024], replicated
- grad_ada: float32 [1024, 6, 1024], P(None, None, 'tensor')
- grad_ada_bias: float32 [6, 1024], P(None, 'tensor')
All inputs are finite; a program needn't handle non-finite values.
Results may differ from a plain program's by a relative error of at most 0.02.
Values may be sent and summed in bfloat16 or wider, within the bound.
No kernel may reach another device: no remote copies, remote signals or barrier semaphores. Data moves between devices by JAX's collectives and lax.ppermute only.
A program may use at most 320 MiB of HBM per device.

v0:
```python
from functools import partial

import jax
import jax.numpy as jnp
from jax import lax
from jax.sharding import PartitionSpec as P

HD = 64


def layer_stats(values):
    row_mean = jnp.mean(values, -1, keepdims=True)
    centered = values - row_mean
    variance = jnp.mean(centered * centered, -1, keepdims=True)
    inverse = lax.rsqrt(variance + 1e-06)
    return (centered * inverse, inverse)


def norm_back(d_norm, normed, inverse):
    first = jnp.mean(d_norm, -1, keepdims=True)
    second = jnp.mean(d_norm * normed, -1, keepdims=True)
    return inverse * (d_norm - first - normed * second)


def shards(
    tokens,
    cond,
    cotangent,
    qkv_weight,
    qv_bias,
    output_projection_weight,
    proj_bias,
    fc1_weight,
    fc1_bias,
    fc2_weight,
    fc2_bias,
    ada_weight,
    ada_bias,
):
    row_count, latents, model_width = tokens.shape
    local_width = qkv_weight.shape[2]
    heads_local = local_width // HD
    seq_len = row_count * lax.axis_size("tensor")
    factor = HD ** (-0.5)

    def to_heads(array):
        return jnp.transpose(array.reshape(seq_len, latents, heads_local, HD), (1, 2, 0, 3))

    def from_heads(array):
        return jnp.transpose(array, (2, 0, 1, 3)).reshape(seq_len, latents, local_width)

    def attend(block):
        query_blk, key_blk, value_blk = block
        scores = (
            jnp.einsum("hqd,hkd->hqk", query_blk, key_blk, preferred_element_type=jnp.float32)
            * factor
        )
        row_max = jnp.max(scores, -1, keepdims=True)
        log_total = row_max + jnp.log(jnp.sum(jnp.exp(scores - row_max), -1, keepdims=True))
        probs = jnp.exp(scores - log_total).astype(jnp.bfloat16)
        result = jnp.einsum("hqk,hkd->hqd", probs, value_blk, preferred_element_type=jnp.float32)
        return (result.astype(jnp.bfloat16), log_total[..., 0])

    def attend_back(block):
        query_blk, key_blk, value_blk, log_total, grad_blk = block
        scores = (
            jnp.einsum("hqd,hkd->hqk", query_blk, key_blk, preferred_element_type=jnp.float32)
            * factor
        )
        weights = jnp.exp(scores - log_total[..., None])
        d_probs = jnp.einsum(
            "hqd,hkd->hqk", grad_blk, value_blk, preferred_element_type=jnp.float32
        )
        d_scores = (weights * (d_probs - jnp.sum(d_probs * weights, -1, keepdims=True))).astype(
            jnp.bfloat16
        )
        d_query = (
            jnp.einsum("hqk,hkd->hqd", d_scores, key_blk, preferred_element_type=jnp.float32)
            * factor
        ).astype(jnp.bfloat16)
        d_key = (
            jnp.einsum("hqk,hqd->hkd", d_scores, query_blk, preferred_element_type=jnp.float32)
            * factor
        ).astype(jnp.bfloat16)
        d_value = jnp.einsum(
            "hqk,hqd->hkd",
            weights.astype(jnp.bfloat16),
            grad_blk,
            preferred_element_type=jnp.float32,
        ).astype(jnp.bfloat16)
        return (d_query, d_key, d_value)

    cond_float = cond.astype(jnp.float32)
    silu_c = jax.nn.silu(cond_float).astype(jnp.bfloat16)
    ada_flat = ada_weight.reshape(model_width, 6 * local_width)
    mod_part = jnp.dot(silu_c, ada_flat, preferred_element_type=jnp.float32) + ada_bias.reshape(
        6 * local_width
    ).astype(jnp.float32)
    mod_part = mod_part.reshape(latents, 6, local_width).astype(jnp.bfloat16)
    modulation = lax.all_gather(mod_part, "tensor", axis=2, tiled=True).astype(jnp.float32)
    shift1, scale1, gate1, shift2, scale2, gate2 = [
        modulation[:, index][None] for index in range(6)
    ]
    first_dense_weight_gathered, second_dense_weight_gathered, fc1_bias_full = (
        lax.all_gather(fc1_weight, "tensor", axis=1, tiled=True),
        lax.all_gather(fc2_weight, "tensor", axis=0, tiled=True),
        lax.all_gather(fc1_bias, "tensor", axis=0, tiled=True),
    )
    inputs_float = tokens.astype(jnp.float32)
    norm1, inverse1 = layer_stats(inputs_float)
    attn_in = (norm1 * (1.0 + scale1) + shift1).astype(jnp.bfloat16)
    attention_gathered = lax.all_gather(attn_in, "tensor", axis=0, tiled=True)
    query_key_value_rows = qkv_weight.reshape(model_width, 3 * local_width)
    projected = jnp.einsum(
        "rap,po->rao", attention_gathered, query_key_value_rows, preferred_element_type=jnp.float32
    ).reshape(seq_len, latents, 3, local_width)
    bias_float = qv_bias.astype(jnp.float32)
    queries = to_heads((projected[:, :, 0] + bias_float[0]).astype(jnp.bfloat16))
    keys_all = to_heads(projected[:, :, 1].astype(jnp.bfloat16))
    values_all = to_heads((projected[:, :, 2] + bias_float[1]).astype(jnp.bfloat16))
    attended_heads, log_totals = lax.map(attend, (queries, keys_all, values_all))
    attention_result = from_heads(attended_heads)
    shard_slice = attention_result
    attn_out = lax.psum_scatter(
        jnp.einsum(
            "pac,cx->pax", shard_slice, output_projection_weight, preferred_element_type=jnp.float32
        ).astype(jnp.bfloat16),
        "tensor",
        scatter_dimension=0,
        tiled=True,
    ).astype(jnp.float32) + proj_bias.astype(jnp.float32)
    mid = inputs_float + gate1 * attn_out
    norm2, inverse2 = layer_stats(mid)
    feedforward_input = (norm2 * (1.0 + scale2) + shift2).astype(jnp.bfloat16)
    pre = jnp.einsum(
        "biw,wr->bir",
        feedforward_input,
        first_dense_weight_gathered,
        preferred_element_type=jnp.float32,
    ) + fc1_bias_full.astype(jnp.float32)
    gelu_activation = jax.nn.gelu(pre, approximate=True).astype(jnp.bfloat16)
    mlp_out = jnp.einsum(
        "gzw,wt->gzt",
        gelu_activation,
        second_dense_weight_gathered,
        preferred_element_type=jnp.float32,
    ) + fc2_bias.astype(jnp.float32)
    output = (mid + gate2 * mlp_out).astype(jnp.bfloat16)
    grad_out = cotangent.astype(jnp.float32)
    grad_gate2 = jnp.sum(grad_out * mlp_out, 0)
    feedforward_gradient = (grad_out * gate2).astype(jnp.bfloat16)
    fc2_bias_part = jnp.sum(feedforward_gradient.astype(jnp.float32), (0, 1))
    second_dense_gradient_shard = jnp.einsum(
        "rqu,rqf->uf", gelu_activation, feedforward_gradient, preferred_element_type=jnp.float32
    )
    activation_gradient = jnp.einsum(
        "zqy,vy->zqv",
        feedforward_gradient,
        second_dense_weight_gathered,
        preferred_element_type=jnp.float32,
    )
    gelu_pull = jax.vjp(partial(jax.nn.gelu, approximate=True), pre)[1]
    preactivation_gradient = gelu_pull(activation_gradient)[0].astype(jnp.bfloat16)
    fc1_bias_part = jnp.sum(preactivation_gradient.astype(jnp.float32), (0, 1))
    first_dense_gradient_shard = jnp.einsum(
        "hic,hip->cp", feedforward_input, preactivation_gradient, preferred_element_type=jnp.float32
    )
    feedforward_input_gradient = jnp.einsum(
        "xfg,yg->xfy",
        preactivation_gradient,
        first_dense_weight_gathered,
        preferred_element_type=jnp.float32,
    )
    grad_fc1, grad_fc2, grad_fc1_bias = (
        lax.psum_scatter(
            first_dense_gradient_shard.astype(jnp.bfloat16),
            "tensor",
            scatter_dimension=1,
            tiled=True,
        ).astype(jnp.float32),
        lax.psum_scatter(
            second_dense_gradient_shard.astype(jnp.bfloat16),
            "tensor",
            scatter_dimension=0,
            tiled=True,
        ).astype(jnp.float32),
        lax.psum_scatter(
            fc1_bias_part.astype(jnp.bfloat16), "tensor", scatter_dimension=0, tiled=True
        ).astype(jnp.float32),
    )
    grad_shift2 = jnp.sum(feedforward_input_gradient, 0)
    grad_scale2 = jnp.sum(feedforward_input_gradient * norm2, 0)
    d_mid = grad_out + norm_back(feedforward_input_gradient * (1.0 + scale2), norm2, inverse2)
    grad_gate1 = jnp.sum(d_mid * attn_out, 0)
    d_attn = (d_mid * gate1).astype(jnp.bfloat16)
    proj_bias_part = jnp.sum(d_attn.astype(jnp.float32), (0, 1))
    attention_gathered_gradient = lax.all_gather(d_attn, "tensor", axis=0, tiled=True)
    output_projection_gradient = jnp.einsum(
        "pti,ptq->iq",
        attention_result,
        attention_gathered_gradient,
        preferred_element_type=jnp.float32,
    )
    d_attended = jnp.einsum(
        "btw,vw->btv",
        attention_gathered_gradient,
        output_projection_weight,
        preferred_element_type=jnp.float32,
    ).astype(jnp.bfloat16)
    d_query_h, d_key_h, d_value_h = lax.map(
        attend_back, (queries, keys_all, values_all, log_totals, to_heads(d_attended))
    )
    d_queries = from_heads(d_query_h)
    d_values = from_heads(d_value_h)
    query_key_value_gradient = jnp.stack([d_queries, from_heads(d_key_h), d_values], 2).reshape(
        seq_len, latents, 3 * local_width
    )
    grad_qv_bias = jnp.stack(
        [
            jnp.sum(d_queries.astype(jnp.float32), (0, 1)),
            jnp.sum(d_values.astype(jnp.float32), (0, 1)),
        ],
        0,
    )
    grad_qkv = jnp.einsum(
        "iyz,iyn->zn",
        attention_gathered,
        query_key_value_gradient,
        preferred_element_type=jnp.float32,
    ).reshape(model_width, 3, local_width)
    shard_slice = query_key_value_gradient
    d_attn_in = lax.psum_scatter(
        jnp.einsum(
            "rnt,mt->rnm", shard_slice, query_key_value_rows, preferred_element_type=jnp.float32
        ).astype(jnp.bfloat16),
        "tensor",
        scatter_dimension=0,
        tiled=True,
    ).astype(jnp.float32)
    grad_shift1 = jnp.sum(d_attn_in, 0)
    grad_scale1 = jnp.sum(d_attn_in * norm1, 0)
    grad_tokens = d_mid + norm_back(d_attn_in * (1.0 + scale1), norm1, inverse1)
    d_modulation = jnp.stack(
        [grad_shift1, grad_scale1, grad_gate1, grad_shift2, grad_scale2, grad_gate2], 1
    )
    d_mod_local = lax.psum_scatter(
        d_modulation.astype(jnp.bfloat16), "tensor", scatter_dimension=2, tiled=True
    ).astype(jnp.float32)
    grad_ada_bias = jnp.sum(d_mod_local, 0)
    d_mod_flat = d_mod_local.reshape(latents, 6 * local_width)
    grad_ada = jnp.dot(
        silu_c.astype(jnp.float32).T, d_mod_flat, precision=lax.Precision.HIGHEST
    ).reshape(model_width, 6, local_width)
    d_silu_part = jnp.dot(
        d_mod_flat, ada_flat.astype(jnp.float32).T, precision=lax.Precision.HIGHEST
    )
    d_silu, grad_fc2_bias, grad_proj_bias = (
        lax.psum(d_silu_part.astype(jnp.bfloat16), "tensor").astype(jnp.float32),
        lax.psum(fc2_bias_part.astype(jnp.bfloat16), "tensor").astype(jnp.float32),
        lax.psum(proj_bias_part.astype(jnp.bfloat16), "tensor").astype(jnp.float32),
    )
    silu_pull = jax.vjp(jax.nn.silu, cond_float)[1]
    grad_cond = silu_pull(d_silu)[0]
    (
        grad_qkv,
        grad_qv_bias,
        output_projection_gradient,
        grad_proj_bias,
        grad_fc1,
        grad_fc1_bias,
        grad_fc2,
        grad_fc2_bias,
        grad_ada,
        grad_ada_bias,
    ) = (
        lax.psum(grad_qkv.astype(jnp.bfloat16), "dp").astype(jnp.float32),
        lax.psum(grad_qv_bias.astype(jnp.bfloat16), "dp").astype(jnp.float32),
        lax.psum(output_projection_gradient.astype(jnp.bfloat16), "dp").astype(jnp.float32),
        lax.psum(grad_proj_bias.astype(jnp.bfloat16), "dp").astype(jnp.float32),
        lax.psum(grad_fc1.astype(jnp.bfloat16), "dp").astype(jnp.float32),
        lax.psum(grad_fc1_bias.astype(jnp.bfloat16), "dp").astype(jnp.float32),
        lax.psum(grad_fc2.astype(jnp.bfloat16), "dp").astype(jnp.float32),
        lax.psum(grad_fc2_bias.astype(jnp.bfloat16), "dp").astype(jnp.float32),
        lax.psum(grad_ada.astype(jnp.bfloat16), "dp").astype(jnp.float32),
        lax.psum(grad_ada_bias.astype(jnp.bfloat16), "dp").astype(jnp.float32),
    )
    return (
        output,
        grad_tokens,
        grad_cond,
        grad_qkv,
        grad_qv_bias,
        output_projection_gradient,
        grad_proj_bias,
        grad_fc1,
        grad_fc1_bias,
        grad_fc2,
        grad_fc2_bias,
        grad_ada,
        grad_ada_bias,
    )


def solution(mesh):
    return jax.shard_map(
        shards,
        mesh=mesh,
        in_specs=(
            P("tensor", "dp", None),
            P("dp", None),
            P("tensor", "dp", None),
            P(None, None, "tensor"),
            P(None, "tensor"),
            P("tensor", None),
            P(),
            P(None, "tensor"),
            P("tensor"),
            P("tensor", None),
            P(),
            P(None, None, "tensor"),
            P(None, "tensor"),
        ),
        out_specs=(
            P("tensor", "dp", None),
            P("tensor", "dp", None),
            P("dp", None),
            P(None, None, "tensor"),
            P(None, "tensor"),
            P("tensor", None),
            P(),
            P(None, "tensor"),
            P("tensor"),
            P("tensor", None),
            P(),
            P(None, None, "tensor"),
            P(None, "tensor"),
        ),
        check_vma=False,
    )
```

profile of v0, /device:TPU:0, one launch (start us, length us, event | category | flops | bytes accessed | tf_op | source)
XLA Modules:
  0.0 2937.0 jit_solution(14725982527945998863)
XLA Ops:
  54.5 285.8 %all-gather.5.cloned.1.call-done = bf16[1024,8,1024]{2,0,1:T(8,128)(2,1)} async-done(((bf16[256,8,1024]{2,0,1:T(8,128)(2,1)}), bf16[1024,8,1024]{2,0,1:T(8,128)(2,1)}) %all-gather.5.cloned.1.call-update) | async-done | bytes 16777232 | tf_op jit(solution)/shard_map/all_gather | solution.py:112
  340.3 21.8 fusion.63
  382.3 225.3 %while.26 = (s32[]{:T(128)}, bf16[8,4,1024,64]{2,3,1,0:T(8,128)(2,1)}, f32[8,4,1024]{2,1,0:T(4,128)}, bf16[8,4,1024,64]{2,3,1,0:T(8,128)(2,1)}, bf16[8,4,1024,64...) while((s32[]{:T(128)}, bf16[8,4,1024,64]{2,3,1,0:T(8,128)(2,1)}, ...), condition=%wide.region_5.6_spmd, body=%wide.region_2.5_spmd.sunk | while | flops 1107554304 | bytes 52562008 | solution.py:121
  631.5 265.3 %reduce-scatter.6.cloned.1.call-done = bf16[256,8,1024]{2,0,1:T(8,128)(2,1)} async-done(((bf16[1024,8,1024]{2,0,1:T(8,128)(2,1)}), bf16[256,8,1024]{2,0,1:T(8,128)(2,1)}) %reduce-scatter.6.cloned.1.call-update) | async-done | bytes 4194320 | tf_op jit(solution)/shard_map/reduce_scatter | solution.py:124
  909.9 139.0 %all-gather.7.cloned.1.call-done = bf16[1024,4096]{1,0:T(8,128)(2,1)} async-done(((bf16[1024,1024]{1,0:T(8,128)(2,1)}), bf16[1024,4096]{1,0:T(8,128)(2,1)}) %all-gather.7.cloned.1.call-update) | async-done | bytes 8388624 | tf_op jit(solution)/shard_map/all_gather | solution.py:105
  1048.8 39.2 %multiply_convert_fusion.1 = (bf16[256,8,4096]{2,0,1:T(8,128)(2,1)}, f32[256,8,4096]{2,0,1:T(8,128)}) fusion(f32[4096]{0:T(1024)S(1)} %convert_element_type.211, bf16[1024,4096]{1,0:T(8,128)(2,1)} %all-gather.7.cloned.1.call-done, f32[8,1024]{1,0:T(8,128)S(1)} %get-tuple-element.209, f32[8,1024]{1,0:T(8,128)S(1)} %get-tuple-element.210, ...), kind=kOutput, calls=%fused_computation.68 | convolution fusion | flops 17284726784 | bytes 67244032 | tf_op jit(solution)/shard_map/biw,wr->bir/dot_general | solution.py:135
  1088.0 110.2 %all-gather.9.cloned.1.call-done = bf16[4096,1024]{1,0:T(8,128)(2,1)} async-done(((bf16[1024,1024]{1,0:T(8,128)(2,1)}), bf16[4096,1024]{1,0:T(8,128)(2,1)}) %all-gather.9.cloned.1.call-update) | async-done | bytes 8388624 | tf_op jit(solution)/shard_map/all_gather | solution.py:106
  1198.2 24.6 fusion.85
  1222.8 49.9 %fusion.126 = (bf16[4096]{0:T(1024)(128)(2,1)}, bf16[256,8,4096]{2,0,1:T(8,128)(2,1)}) fusion(f32[256,8,4096]{2,0,1:T(8,128)} %get-tuple-element.215, f32[4096]{0:T(1024)S(1)} %convert_element_type.211, bf16[4096,1024]{1,0:T(8,128)(2,1)} %all-gather.9.cloned.1.call-done, f32[8,1024]{1,0:T(8,128)S(1)} %copy-done.26, bf16[256,8,1024]{2,1,0:T(8,128)(2,1)S(1)} %copy-done.8), kind=kOutput, calls=%fused_computation.185 | convolution fusion | flops 17370705920 | bytes 62971904 | tf_op jit(solution)/shard_map/zqy,vy->zqv/dot_general | solution.py:156
  1272.7 42.1 %multiply_reduce_fusion.2 = (bf16[8,1024]{1,0:T(8,128)(2,1)}, f32[256,8]{0,1:T(8,128)S(1)}, f32[256,8]{0,1:T(8,128)S(1)}, bf16[8,1024]{1,0:T(8,128)(2,1)}, bf16[...) fusion(f32[256,8]{0,1:T(8,128)S(1)} %add_rsqrt_fusion, ...), kind=kOutput, calls=%fused_computation.112 | convolution fusion | flops 17223880704 | bytes 58908672 | tf_op jit(solution)/shard_map/xfg,yg->xfy/dot_general | solution.py:168
  1314.8 16.3 fusion.124
  1331.2 285.1 %all-gather.11.cloned.1.call-done = bf16[1024,8,1024]{2,0,1:T(8,128)(2,1)} async-done(((bf16[256,8,1024]{2,0,1:T(8,128)(2,1)}), bf16[1024,8,1024]{2,0,1:T(8,128)(2,1)}) %all-gather.11.cloned.1.call-update) | async-done | bytes 16777232 | tf_op jit(solution)/shard_map/all_gather | solution.py:197
  1616.3 18.4 convolution_convert_fusion.1
  1642.2 458.7 %while.27 = (s32[]{:T(128)}, bf16[8,4,1024,64]{2,3,1,0:T(8,128)(2,1)}, bf16[8,4,1024,64]{2,3,1,0:T(8,128)(2,1)}, bf16[8,4,1024,64]{2,3,1,0:T(8,128)(2,1)}, bf16[...) while((s32[]{:T(128)}, ...), condition=%wide.region_13.14_spmd, body=%wide.region_11.13_spmd.sunk | while | flops 2735992832 | bytes 231855296 | solution.py:210
  2120.2 20.0 bitcast_convert_fusion
  2140.3 278.6 %reduce-scatter.8.cloned.1.call-done = bf16[256,8,1024]{2,0,1:T(8,128)(2,1)} async-done(((bf16[1024,8,1024]{2,0,1:T(8,128)(2,1)}), bf16[256,8,1024]{2,0,1:T(8,128)(2,1)}) %reduce-scatter.8.cloned.1.call-update) | async-done | bytes 4194320 | tf_op jit(solution)/shard_map/reduce_scatter | solution.py:232
  2445.2 29.7 %bitcast_convert_fusion.2 = bf16[1024,4096]{1,0:T(8,128)(2,1)} fusion(bf16[256,8,4096]{2,0,1:T(8,128)(2,1)} %get-tuple-element.218, f32[8,1024]{1,0:T(8,128)S(1)} %copy-done.39, f32[8,1024]{1,0:T(8,128)S(1)} %copy-done.29, f32[256,8]{0,1:T(8,128)S(1)} %copy-done.37, f32[256,8]{0,1:T(8,128)S(1)} %copy-done.35, ...), kind=kOutput, calls=%fused_computation.74 | convolution fusion | flops 17205035008 | bytes 33673216 | tf_op jit(solution)/shard_map/hic,hip->cp/dot_general | solution.py:165
  2475.7 28.7 bitcast_convert_fusion.1
  2517.0 22.2 bitcast_convert_fusion.3
  2542.7 77.6 %reduce-scatter.12.cloned.1.call-done = bf16[1024,1024]{1,0:T(8,128)(2,1)} async-done(((bf16[1024,4096]{1,0:T(8,128)(2,1)}), bf16[1024,1024]{1,0:T(8,128)(2,1)}) %reduce-scatter.12.cloned.1.call-update) | async-done | bytes 2097168 | tf_op jit(solution)/shard_map/reduce_scatter | solution.py:175
  2620.3 147.7 %reduce-scatter.14.cloned.1.call-done = bf16[1024,1024]{1,0:T(8,128)(2,1)} async-done(((bf16[4096,1024]{1,0:T(8,128)(2,1)}), bf16[1024,1024]{1,0:T(8,128)(2,1)}) %reduce-scatter.14.cloned.1.call-update) | async-done | bytes 2097168 | tf_op jit(solution)/shard_map/reduce_scatter | solution.py:181
  2792.8 18.9 all-reduce.3
  2811.8 23.0 all-reduce.1
  2838.5 75.9 %all-reduce.6.cloned.1.call-done = (bf16[1024,3,256]{2,0,1:T(8,128)(2,1)}, bf16[256,1024]{1,0:T(8,128)(2,1)}, bf16[1024,1024]{1,0:T(8,128)(2,1)}, bf16[1024,1024]{1,0:T(8,128)(2,1)}, bf16[1024,6,256]{2,0,1:T(8,128)(2,1)}) async-done(((bf16[1024,3,256]{2,0,1:T(8,128)(2,1)}, bf16[256,1024]{1,0:T(8,128)(2,1)}, bf16[1024,1024]{1,0:T(8,128)(2,1)}, bf16[1024,1024]{1,0:T(8,128)(2,1)}, ...) | async-done | bytes 9437200 | tf_op jit(solution)/shard_map/psum | solution.py:276
  (312 shorter events, 900.9 us)
Async XLA Ops:
  7.2 600.4 %copy-start = (bf16[256,1024]{1,0:T(8,128)(2,1)S(1)}, bf16[256,1024]{1,0:T(8,128)(2,1)}, u32[]{:S(2)}) copy-start(bf16[256,1024]{1,0:T(8,128)(2,1)} %param.22) | copy-start | bytes 1572868
  7.2 333.1 %all-gather.5.cloned.1.call-start = ((), (), s32[]{:S(2)}) async-start(), calls=%async_computation.5 | async-start | bytes 20971520 | tf_op jit(solution)/shard_map/all_gather | solution.py:112
  14.7 37.5 %copy-start.21 = (f32[256,8]{0,1:T(8,128)}, f32[256,8]{0,1:T(8,128)S(1)}, u32[]{:S(2)}) copy-start(f32[256,8]{0,1:T(8,128)S(1)} %broadcast_multiply_fusion.5) | copy-start | bytes 24580
  20.4 31.8 %copy-start.30 = (f32[256,8]{0,1:T(8,128)}, f32[256,8]{0,1:T(8,128)S(1)}, u32[]{:S(2)}) copy-start(f32[256,8]{0,1:T(8,128)S(1)} %add_rsqrt_fusion.1) | copy-start | bytes 24580
  43.6 1005.2 %copy-start.38 = (f32[8,1024]{1,0:T(8,128)}, f32[8,1024]{1,0:T(8,128)S(1)}, u32[]{:S(2)}) copy-start(f32[8,1024]{1,0:T(8,128)S(1)} %get-tuple-element.209) | copy-start | bytes 98308
  43.6 1271.1 %copy-start.16 = (f32[8,1024]{1,0:T(8,128)}, f32[8,1024]{1,0:T(8,128)S(1)}, u32[]{:S(2)}) copy-start(f32[8,1024]{1,0:T(8,128)S(1)} %get-tuple-element.213) | copy-start | bytes 98308
  43.7 1271.1 %copy-start.28 = (f32[8,1024]{1,0:T(8,128)}, f32[8,1024]{1,0:T(8,128)S(1)}, u32[]{:S(2)}) copy-start(f32[8,1024]{1,0:T(8,128)S(1)} %get-tuple-element.210) | copy-start | bytes 98308
  52.2 844.5 %reduce-scatter.6.cloned.1.call-start = ((), (), s32[]{:S(2)}) async-start(), calls=%async_computation.6 | async-start | bytes 20971520 | tf_op jit(solution)/shard_map/reduce_scatter | solution.py:124
  618.1 430.8 %all-gather.7.cloned.1.call-start = ((), (), s32[]{:S(2)}) async-start(), calls=%async_computation.7 | async-start | bytes 10485760 | tf_op jit(solution)/shard_map/all_gather | solution.py:105
  618.8 579.4 %all-gather.9.cloned.1.call-start = ((), (), s32[]{:S(2)}) async-start(), calls=%async_computation.8 | async-start | bytes 10485760 | tf_op jit(solution)/shard_map/all_gather | solution.py:106
  619.4 996.9 %all-gather.11.cloned.1.call-start = ((), (), s32[]{:S(2)}) async-start(), calls=%async_computation.9 | async-start | bytes 20971520 | tf_op jit(solution)/shard_map/all_gather | solution.py:197
  619.5 695.3 %copy-start.32 = (f32[1024]{0:T(1024)}, f32[1024]{0:T(1024)S(1)}, u32[]{:S(2)}) copy-start(f32[1024]{0:T(1024)S(1)} %convert_element_type.209) | copy-start | bytes 12292
  904.4 410.4 %copy-start.34 = (f32[256,8]{0,1:T(8,128)}, f32[256,8]{0,1:T(8,128)S(1)}, u32[]{:S(2)}) copy-start(f32[256,8]{0,1:T(8,128)S(1)} %broadcast_multiply_fusion.4) | copy-start | bytes 24580
  909.9 404.9 %copy-start.36 = (f32[256,8]{0,1:T(8,128)}, f32[256,8]{0,1:T(8,128)S(1)}, u32[]{:S(2)}) copy-start(f32[256,8]{0,1:T(8,128)S(1)} %add_rsqrt_fusion) | copy-start | bytes 24580
  1331.1 1087.8 %reduce-scatter.8.cloned.1.call-start = ((), (), s32[]{:S(2)}) async-start(), calls=%async_computation.10 | async-start | bytes 20971520 | tf_op jit(solution)/shard_map/reduce_scatter | solution.py:232
  2140.2 278.7 %copy-start.19 = (f32[8,1024]{1,0:T(8,128)S(1)}, f32[8,1024]{1,0:T(8,128)}, u32[]{:S(2)}) copy-start(f32[8,1024]{1,0:T(8,128)} %copy-done.18) | copy-start | bytes 98308
  2140.2 278.7 %copy-start.22 = (f32[256,8]{0,1:T(8,128)S(1)}, f32[256,8]{0,1:T(8,128)}, u32[]{:S(2)}) copy-start(f32[256,8]{0,1:T(8,128)} %copy-done.21) | copy-start | bytes 24580
  2140.3 278.7 %copy-start.31 = (f32[256,8]{0,1:T(8,128)S(1)}, f32[256,8]{0,1:T(8,128)}, u32[]{:S(2)}) copy-start(f32[256,8]{0,1:T(8,128)} %copy-done.30) | copy-start | bytes 24580
  2140.3 290.2 %copy-start.33 = (f32[1024]{0:T(1024)S(1)}, f32[1024]{0:T(1024)}, u32[]{:S(2)}) copy-start(f32[1024]{0:T(1024)} %copy-done.32) | copy-start | bytes 12292
  2140.3 399.0 %reduce-scatter.10.cloned.1.call-start = ((), (), s32[]{:S(2)}) async-start(), calls=%async_computation.11 | async-start | bytes 122880 | tf_op jit(solution)/shard_map/reduce_scatter | solution.py:246
  2445.1 175.2 %reduce-scatter.12.cloned.1.call-start = ((), (), s32[]{:S(2)}) async-start(), calls=%async_computation.12 | async-start | bytes 10485760 | tf_op jit(solution)/shard_map/reduce_scatter | solution.py:175
  2475.0 293.1 %reduce-scatter.14.cloned.1.call-start = ((), (), s32[]{:S(2)}) async-start(), calls=%async_computation.13 | async-start | bytes 10485760 | tf_op jit(solution)/shard_map/reduce_scatter | solution.py:181
  2504.4 409.9 %all-reduce.6.cloned.1.call-start = ((), (), s32[]{:S(2)}) async-start(), calls=%async_computation.14 | async-start | bytes 18874368 | tf_op jit(solution)/shard_map/psum | solution.py:276
  2539.2 228.8 %copy-start.50 = (u32[32]{0:T(128)S(1)}, u32[32]{0:T(128)}, u32[]{:S(2)}) copy-start(u32[32]{0:T(128)} %constant.83) | copy-start | bytes 388
  (51 other events, 621.6 us)
Sparse Core Ops, SparseCore 0:
  52.4 287.8 all-gather.4
  618.2 278.5 reduce-scatter.5
  898.4 150.3 all-gather.6
  1050.3 147.8 all-gather.8
  1331.2 284.9 all-gather.10
  2140.4 278.4 reduce-scatter.7
  2445.2 19.8 reduce-scatter.9
  2475.1 145.1 reduce-scatter.11
  2622.8 145.1 reduce-scatter.13
  2774.0 140.3 all-reduce.5
where the time goes:
time: 2950 us; the launch traced here: 2940 us
  waiting for transfers between devices  1670 us (57%)
  matrix products  825 us (28%)
  other arithmetic  261 us (9%)
  local copies, waits for them, and re-layouts  98.3 us (3%)
  blocking collectives  69 us (2%)
    all_gather x1, waiting for transfers between devices, shards(): attention_gathered = lax.all_gather(attn_in, 'tensor', axis=0, tiled=True)  286 us
    all_gather x1, waiting for transfers between devices, shards(): lax.all_gather(d_attn, 'tensor', axis=0, tiled=True)  285 us
    reduce_scatter x1, waiting for transfers between devices, shards(): lax.psum_scatter(jnp.einsum('rnt,mt->rnm', shard_slice, query_key_value_r...  279 us
    reduce_scatter x1, waiting for transfers between devices, shards(): lax.psum_scatter(jnp.einsum('pac,cx->pax', shard_slice, output_projection...  265 us
    reduce_scatter x1, waiting for transfers between devices, shards(): lax.psum_scatter(second_dense_gradient_shard.astype(jnp.bfloat16), 'tenso...  148 us
    all_gather x1, waiting for transfers between devices, shards(): lax.all_gather(fc1_weight, 'tensor', axis=1, tiled=True)  139 us
    dot_general x8, matrix products, attend_back(): jnp.einsum('hqd,hkd->hqk', grad_blk, value_blk, preferred_element_type=jn...  112 us
    all_gather x1, waiting for transfers between devices, shards(): lax.all_gather(fc2_weight, 'tensor', axis=0, tiled=True)  110 us
  transfers between devices with their start and end apart: 10, of which 9 were waited for; matrix products, arithmetic and copies ran while one was open for 6% of the time, Pallas kernels for 0%

commit v1 on v0

--- a/solution.py
+++ b/solution.py
@@ -3,9 +3,12 @@
 import jax
 import jax.numpy as jnp
 from jax import lax
+from jax.experimental import pallas as pl
+from jax.experimental.pallas import tpu as pltpu
 from jax.sharding import PartitionSpec as P
 
 HD = 64
+LANES = 128
 
 
 def layer_stats(values):
@@ -22,7 +25,7 @@
     return inverse * (d_norm - first - normed * second)
 
 
-def shards(
+def split_heads(
     tokens,
     cond,
     cotangent,
@@ -301,6 +304,389 @@
     )
 
 
+def _nt(left, right):
+    return lax.dot_general(
+        left, right, (((1,), (1,)), ((), ())), preferred_element_type=jnp.float32
+    )
+
+
+def _attend_kernel(qkv_ref, out_ref, lse_ref, *, width, rows):
+    lane = lax.broadcasted_iota(jnp.int32, (1, LANES), 1)
+    first = lane < HD
+
+    def chunk(index, carry):
+        at = pl.ds(pl.multiple_of(index * rows, rows), rows)
+        totals = jnp.zeros((rows, LANES), jnp.float32)
+        for pair in range(width // LANES):
+            lo = pair * LANES
+            query = qkv_ref[at, lo : lo + LANES] * jnp.bfloat16(HD**-0.5)
+            key = qkv_ref[:, width + lo : width + lo + LANES]
+            value = qkv_ref[:, 2 * width + lo : 2 * width + lo + LANES]
+            parts = []
+            for side in range(2):
+                mine = first if side == 0 else jnp.logical_not(first)
+                scores = _nt(jnp.where(mine, query, 0), key)
+                top = jnp.max(scores, -1, keepdims=True)
+                weights = jnp.exp(scores - top).astype(jnp.bfloat16)
+                mixed = jnp.dot(
+                    weights, jnp.where(mine, value, 1), preferred_element_type=jnp.float32
+                )
+                other = HD * (1 - side)
+                total = mixed[:, other : other + 1]
+                parts.append(mixed / total)
+                totals = jnp.where(lane == 2 * pair + side, top + jnp.log(total), totals)
+            out_ref[at, lo : lo + LANES] = jnp.where(first, parts[0], parts[1]).astype(
+                jnp.bfloat16
+            )
+        lse_ref[at, :] = totals
+        return carry
+
+    lax.fori_loop(0, qkv_ref.shape[0] // rows, chunk, 0)
+
+
+def attend(qkv, latents, groups, width, seq):
+    heads = groups * (width // HD)
+    work = latents * heads * seq * seq
+    return pl.pallas_call(
+        partial(_attend_kernel, width=width, rows=min(256, seq)),
+        grid=(latents, groups),
+        in_specs=[pl.BlockSpec((seq, 3 * width), lambda i, j: (i, j))],
+        out_specs=[
+            pl.BlockSpec((seq, width), lambda i, j: (i, j)),
+            pl.BlockSpec((seq, LANES), lambda i, j: (i, j)),
+        ],
+        out_shape=[
+            jax.ShapeDtypeStruct((latents * seq, groups * width), jnp.bfloat16),
+            jax.ShapeDtypeStruct((latents * seq, groups * LANES), jnp.float32),
+        ],
+        compiler_params=pltpu.CompilerParams(vmem_limit_bytes=40 * 2**20),
+        cost_estimate=pl.CostEstimate(
+            flops=16 * HD * work,
+            bytes_accessed=latents * seq * groups * (8 * width + 4 * LANES),
+            transcendentals=work,
+        ),
+        name="attend",
+    )(qkv)
+
+
+def _split3(column):
+    high = column.astype(jnp.bfloat16).astype(jnp.float32)
+    middle = (column - high).astype(jnp.bfloat16).astype(jnp.float32)
+    return (high, middle, column - high - middle)
+
+
+def _attend_back_kernel(qkv_ref, out_ref, lse_ref, grad_ref, dqkv_ref, *, width, rows):
+    seq = qkv_ref.shape[0]
+    lane = lax.broadcasted_iota(jnp.int32, (1, LANES), 1)
+    first = lane < HD
+    scale = jnp.bfloat16(HD**-0.5)
+
+    def extend(mine, base, array, column):
+        high, middle, low = _split3(column)
+        extra = jnp.where(
+            lane == base,
+            high,
+            jnp.where(lane == base + 1, middle, jnp.where(lane == base + 2, low, 0.0)),
+        )
+        return jnp.where(mine, array, extra.astype(jnp.bfloat16))
+
+    for pair in range(width // LANES):
+        lo = pair * LANES
+        query = qkv_ref[:, lo : lo + LANES] * scale
+        grad = grad_ref[:, lo : lo + LANES]
+        product = grad.astype(jnp.float32) * out_ref[:, lo : lo + LANES].astype(jnp.float32)
+        queries, grads = [], []
+        for side in range(2):
+            mine = first if side == 0 else jnp.logical_not(first)
+            base = HD * (1 - side)
+            head = 2 * pair + side
+            queries.append(extend(mine, base, query, -lse_ref[:, head : head + 1]))
+            inner = jnp.sum(jnp.where(mine, product, 0.0), -1, keepdims=True)
+            grads.append(extend(mine, base, grad, -inner))
+        d_query = [jnp.zeros((HD, seq), jnp.float32)] * 2
+        for index in range(seq // rows):
+            at = slice(index * rows, (index + 1) * rows)
+            key = qkv_ref[at, width + lo : width + lo + LANES]
+            value = qkv_ref[at, 2 * width + lo : 2 * width + lo + LANES]
+            key_t = key.T
+            d_key, d_value = [], []
+            for side in range(2):
+                mine = first if side == 0 else jnp.logical_not(first)
+                base = HD * (1 - side)
+                ones = jnp.where((lane >= base) & (lane < base + 3), 1.0, 0.0).astype(jnp.bfloat16)
+                weights = jnp.exp(_nt(jnp.where(mine, key, ones), queries[side]))
+                d_scores = (
+                    weights * _nt(jnp.where(mine, value, ones), grads[side])
+                ).astype(jnp.bfloat16)
+                d_value.append(
+                    jnp.dot(
+                        weights.astype(jnp.bfloat16), grad, preferred_element_type=jnp.float32
+                    )
+                )
+                d_key.append(jnp.dot(d_scores, query, preferred_element_type=jnp.float32))
+                d_query[side] = d_query[side] + jnp.dot(
+                    key_t[side * HD : (side + 1) * HD],
+                    d_scores,
+                    preferred_element_type=jnp.float32,
+                )
+            dqkv_ref[at, width + lo : width + lo + LANES] = jnp.where(
+                first, d_key[0], d_key[1]
+            ).astype(jnp.bfloat16)
+            dqkv_ref[at, 2 * width + lo : 2 * width + lo + LANES] = jnp.where(
+                first, d_value[0], d_value[1]
+            ).astype(jnp.bfloat16)
+        d_query_t = jnp.concatenate(d_query, 0) * (HD**-0.5)
+        dqkv_ref[:, lo : lo + LANES] = d_query_t.T.astype(jnp.bfloat16)
+
+
+def attend_back(qkv, out, lse, grad, latents, groups, width, seq):
+    heads = groups * (width // HD)
+    work = latents * heads * seq * seq
+    return pl.pallas_call(
+        partial(_attend_back_kernel, width=width, rows=min(256, seq)),
+        grid=(latents, groups),
+        in_specs=[
+            pl.BlockSpec((seq, 3 * width), lambda i, j: (i, j)),
+            pl.BlockSpec((seq, width), lambda i, j: (i, j)),
+            pl.BlockSpec((seq, LANES), lambda i, j: (i, j)),
+            pl.BlockSpec((seq, width), lambda i, j: (i, j)),
+        ],
+        out_specs=pl.BlockSpec((seq, 3 * width), lambda i, j: (i, j)),
+        out_shape=jax.ShapeDtypeStruct(qkv.shape, jnp.bfloat16),
+        compiler_params=pltpu.CompilerParams(vmem_limit_bytes=48 * 2**20),
+        cost_estimate=pl.CostEstimate(
+            flops=40 * HD * work,
+            bytes_accessed=latents * seq * groups * (16 * width + 4 * LANES),
+            transcendentals=work,
+        ),
+        name="attend_back",
+    )(qkv, out, lse, grad)
+
+
+BY_OWNER, BY_SHARE = ("tensor", "dp"), ("dp", "tensor")
+
+
+def exchange(pieces):
+    return lax.all_to_all(pieces, "tensor", 0, 0)
+
+
+def gather_rows(part, order):
+    share = part.shape[0] // lax.axis_size("dp")
+    mine = lax.dynamic_slice_in_dim(part, lax.axis_index("dp") * share, share, 0)
+    return lax.all_gather(mine, order, axis=0, tiled=True)
+
+
+def by_share(rows):
+    groups, shares = lax.axis_size("tensor"), lax.axis_size("dp")
+    split = rows.reshape(groups, shares, -1, *rows.shape[1:])
+    return jnp.swapaxes(split, 0, 1).reshape(rows.shape)
+
+
+def sum_rows(whole):
+    share = lax.psum_scatter(
+        whole.astype(jnp.bfloat16), "dp", scatter_dimension=0, tiled=True
+    )
+    share = lax.psum_scatter(share, "tensor", scatter_dimension=0, tiled=True)
+    return lax.all_gather(share, "dp", axis=0, tiled=True).astype(jnp.float32)
+
+
+def whole_latents(
+    tokens,
+    cond,
+    cotangent,
+    qkv_weight,
+    qv_bias,
+    output_projection_weight,
+    proj_bias,
+    fc1_weight,
+    fc1_bias,
+    fc2_weight,
+    fc2_bias,
+    ada_weight,
+    ada_bias,
+):
+    row_count, group_latents, model_width = tokens.shape
+    groups = lax.axis_size("tensor")
+    latents = group_latents // groups
+    seq = row_count * groups
+    width = qkv_weight.shape[2]
+    hidden = fc1_weight.shape[1]
+    rows = latents * seq
+    me = lax.axis_index("tensor")
+
+    def to_latents(array):
+        pieces = jnp.transpose(
+            array.reshape(row_count, groups, latents, model_width), (1, 2, 0, 3)
+        )
+        return jnp.transpose(exchange(pieces), (1, 0, 2, 3)).reshape(latents, seq, model_width)
+
+    def to_tokens(array):
+        pieces = jnp.transpose(
+            array.reshape(latents, groups, row_count, model_width), (1, 0, 2, 3)
+        )
+        return jnp.transpose(exchange(pieces), (2, 0, 1, 3)).reshape(
+            row_count, group_latents, model_width
+        )
+
+    cond_float = cond.astype(jnp.float32)
+    silu_c = jax.nn.silu(cond_float).astype(jnp.bfloat16)
+    ada_flat = ada_weight.reshape(model_width, 6 * width)
+    mod_part = jnp.dot(silu_c, ada_flat, preferred_element_type=jnp.float32) + ada_bias.reshape(
+        6 * width
+    ).astype(jnp.float32)
+    mod_part = mod_part.reshape(group_latents, 6, width).astype(jnp.bfloat16)
+    modulation = lax.dynamic_slice_in_dim(
+        lax.all_gather(mod_part, "tensor", axis=2, tiled=True), me * latents, latents, 0
+    ).astype(jnp.float32)
+    shift1, scale1, gate1, shift2, scale2, gate2 = [
+        modulation[:, index][:, None] for index in range(6)
+    ]
+
+    qkv_rows = gather_rows(
+        jnp.transpose(qkv_weight, (1, 2, 0)).reshape(3 * width, model_width),
+        BY_OWNER,
+    )
+    inputs_float = to_latents(tokens).astype(jnp.float32)
+    proj_rows = gather_rows(output_projection_weight, BY_OWNER)
+    fc1_rows = gather_rows(fc1_weight.T, BY_SHARE)
+    fc2_rows = gather_rows(fc2_weight, BY_SHARE)
+    fc1_bias_full = by_share(
+        lax.all_gather(fc1_bias, "tensor", axis=0, tiled=True)
+    ).astype(jnp.float32)
+    qv_bias_full = lax.all_gather(qv_bias, "tensor", axis=0).astype(jnp.float32)
+    qkv_bias = jnp.stack(
+        [qv_bias_full[:, 0], jnp.zeros_like(qv_bias_full[:, 0]), qv_bias_full[:, 1]], 1
+    ).reshape(groups * 3 * width)
+    grad_out = to_latents(cotangent).astype(jnp.float32)
+
+    norm1, inverse1 = layer_stats(inputs_float)
+    attn_in = (norm1 * (1.0 + scale1) + shift1).astype(jnp.bfloat16).reshape(rows, model_width)
+    qkv = (_nt(attn_in, qkv_rows) + qkv_bias).astype(jnp.bfloat16)
+    attended, log_totals = attend(qkv, latents, groups, width, seq)
+    attn_out = (
+        jnp.dot(attended, proj_rows, preferred_element_type=jnp.float32)
+        + proj_bias.astype(jnp.float32)
+    ).reshape(latents, seq, model_width)
+    mid = inputs_float + gate1 * attn_out
+    norm2, inverse2 = layer_stats(mid)
+    mlp_in = (norm2 * (1.0 + scale2) + shift2).astype(jnp.bfloat16).reshape(rows, model_width)
+    pre = _nt(mlp_in, fc1_rows) + fc1_bias_full
+    act = jax.nn.gelu(pre, approximate=True).astype(jnp.bfloat16)
+    mlp_out = (
+        jnp.dot(act, fc2_rows, preferred_element_type=jnp.float32) + fc2_bias.astype(jnp.float32)
+    ).reshape(latents, seq, model_width)
+    output = to_tokens((mid + gate2 * mlp_out).astype(jnp.bfloat16))
+
+    grad_gate2 = jnp.sum(grad_out * mlp_out, 1)
+    d_mlp = (grad_out * gate2).astype(jnp.bfloat16).reshape(rows, model_width)
+    fc2_bias_part = jnp.sum(d_mlp.astype(jnp.float32), 0)
+    grad_fc2 = sum_rows(
+        lax.dot_general(act, d_mlp, (((0,), (0,)), ((), ())), preferred_element_type=jnp.float32)
+    )
+    d_act = _nt(d_mlp, fc2_rows)
+    d_pre = jax.vjp(partial(jax.nn.gelu, approximate=True), pre)[1](d_act)[0].astype(jnp.bfloat16)
+    fc1_bias_part = jnp.sum(d_pre.astype(jnp.float32), 0)
+    grad_fc1 = sum_rows(
+        lax.dot_general(d_pre, mlp_in, (((0,), (0,)), ((), ())), preferred_element_type=jnp.float32)
+    ).T
+    d_mlp_in = jnp.dot(d_pre, fc1_rows, preferred_element_type=jnp.float32).reshape(
+        latents, seq, model_width
+    )
+    grad_shift2 = jnp.sum(d_mlp_in, 1)
+    grad_scale2 = jnp.sum(d_mlp_in * norm2, 1)
+    d_mid = grad_out + norm_back(d_mlp_in * (1.0 + scale2), norm2, inverse2)
+    grad_gate1 = jnp.sum(d_mid * attn_out, 1)
+    d_attn = (d_mid * gate1).astype(jnp.bfloat16).reshape(rows, model_width)
+    proj_bias_part = jnp.sum(d_attn.astype(jnp.float32), 0)
+    grad_proj = sum_rows(
+        by_share(
+            lax.dot_general(
+                attended, d_attn, (((0,), (0,)), ((), ())), preferred_element_type=jnp.float32
+            )
+        )
+    )
+    d_attended = _nt(d_attn, proj_rows).astype(jnp.bfloat16)
+    d_qkv = attend_back(qkv, attended, log_totals, d_attended, latents, groups, width, seq)
+    qkv_bias_part = jnp.sum(d_qkv.astype(jnp.float32), 0)
+    grad_qkv = jnp.transpose(
+        sum_rows(
+            by_share(
+                lax.dot_general(
+                    d_qkv, attn_in, (((0,), (0,)), ((), ())), preferred_element_type=jnp.float32
+                )
+            )
+        ).reshape(3, width, model_width),
+        (2, 0, 1),
+    )
+    d_attn_in = jnp.dot(d_qkv, qkv_rows, preferred_element_type=jnp.float32).reshape(
+        latents, seq, model_width
+    )
+    grad_shift1 = jnp.sum(d_attn_in, 1)
+    grad_scale1 = jnp.sum(d_attn_in * norm1, 1)
+    grad_tokens = to_tokens(
+        (d_mid + norm_back(d_attn_in * (1.0 + scale1), norm1, inverse1)).astype(jnp.bfloat16)
+    ).astype(jnp.float32)
+
+    d_modulation = jnp.stack(
+        [grad_shift1, grad_scale1, grad_gate1, grad_shift2, grad_scale2, grad_gate2], 1
+    ).astype(jnp.bfloat16)
+    d_mod_group = lax.all_to_all(d_modulation, "tensor", 2, 0, tiled=True).reshape(
+        group_latents, 6 * width
+    )
+    d_mod_all = lax.all_gather(d_mod_group, "dp", axis=0, tiled=True)
+    cond_all = lax.all_gather(cond, "dp", axis=0, tiled=True)
+    silu_all = jax.nn.silu(cond_all.astype(jnp.float32)).astype(jnp.bfloat16)
+    grad_ada_bias = jnp.sum(d_mod_all.astype(jnp.float32), 0).reshape(6, width)
+    grad_ada = lax.dot_general(
+        silu_all, d_mod_all, (((0,), (0,)), ((), ())), preferred_element_type=jnp.float32
+    ).reshape(model_width, 6, width)
+    d_silu = lax.psum(_nt(d_mod_group, ada_flat).astype(jnp.bfloat16), "tensor").astype(
+        jnp.float32
+    )
+    grad_cond = jax.vjp(jax.nn.silu, cond_float)[1](d_silu)[0]
+
+    biases = lax.psum(
+        jnp.concatenate([fc2_bias_part, proj_bias_part, fc1_bias_part, qkv_bias_part]).astype(
+            jnp.bfloat16
+        ),
+        ("dp", "tensor"),
+    ).astype(jnp.float32)
+    grad_fc2_bias = biases[:model_width]
+    grad_proj_bias = biases[model_width : 2 * model_width]
+    at = 2 * model_width
+    grad_fc1_bias = lax.dynamic_slice_in_dim(
+        biases[at : at + hidden * groups].reshape(-1, groups, hidden // lax.axis_size("dp")),
+        me,
+        1,
+        1,
+    ).reshape(hidden)
+    at = at + hidden * groups
+    grad_qv_bias = lax.dynamic_slice_in_dim(biases, at + me * 3 * width, 3 * width, 0).reshape(
+        3, width
+    )[::2]
+    return (
+        output,
+        grad_tokens,
+        grad_cond,
+        grad_qkv,
+        grad_qv_bias,
+        grad_proj,
+        grad_proj_bias,
+        grad_fc1,
+        grad_fc1_bias,
+        grad_fc2,
+        grad_fc2_bias,
+        grad_ada,
+        grad_ada_bias,
+    )
+
+
+def shards(tokens, cond, cotangent, qkv_weight, *rest):
+    even = tokens.shape[1] % lax.axis_size("tensor") == 0 and qkv_weight.shape[2] % LANES == 0
+    program = whole_latents if even else split_heads
+    return program(tokens, cond, cotangent, qkv_weight, *rest)
+
+
 def solution(mesh):
     return jax.shard_map(
         shards,

time: 2950 us -> 1310 us (0.44)
  waiting for transfers between devices: 1670 us -> 373 us
  matrix products: 825 us -> 279 us
  blocking collectives: 69 us -> 249 us
  other arithmetic: 261 us -> 90.6 us
  Pallas kernels: 0 us -> 168 us
    all_gather x4 -> x7, waiting for transfers between devices: 820 us -> 0.03 us  [the longest x4 0.03 us: gather_rows(): return lax.all_gather(mine, order, axis=0, tiled=True)]
    dot_general x71 -> x15, matrix products: 825 us -> 279 us  [the longest x5 111 us: _nt(): lax.dot_general(left, right, (((1,), (1,)), ((), ())), preferred_element_...]
    reduce_scatter x5 -> x8, waiting for transfers between devices: 769 us -> 258 us  [the longest x4 158 us: sum_rows(): lax.psum_scatter(whole.astype(jnp.bfloat16), 'dp', scatter_dimension=0, t...]
    pallas_call x0 -> x2, Pallas kernels: none -> 168 us  [the longest x1 98.1 us: attend_back(): pl.pallas_call(partial(_attend_back_kernel, width=width, rows=min(256, se...]
    all_gather x2 -> x6, blocking collectives: 27 us -> 153 us  [the longest x1 71.4 us: whole_latents(): qv_bias_full = lax.all_gather(qv_bias, 'tensor', axis=0).astype(jnp.float32)]
    all_to_all x0 -> x5, waiting for transfers between devices: none -> 115 us  [the longest x4 115 us: exchange(): return lax.all_to_all(pieces, 'tensor', 0, 0)]
    reduce_sum x15 -> x4, other arithmetic: 113 us -> 20.3 us  [the longest x1 10.6 us: whole_latents(): proj_bias_part = jnp.sum(d_attn.astype(jnp.float32), 0)]
    convert_element_type x24 -> x10, other arithmetic: 111 us -> 24.3 us  [the longest x1 5.47 us: whole_latents(): d_mlp = (grad_out * gate2).astype(jnp.bfloat16).reshape(rows, model_width)]
  transfers between devices with their start and end apart: 10 -> 20, of which waited for: 9 -> 7; matrix products, arithmetic and copies ran while one was open for 6% -> 21% of each run, Pallas kernels for 0% -> 5%
where the time goes in v1:
time: 1310 us; the launch traced here: 1300 us
  waiting for transfers between devices  373 us (28%)
  matrix products  279 us (21%)
  blocking collectives  249 us (19%)
  Pallas kernels  168 us (13%)
  local copies, waits for them, and re-layouts  103 us (8%)
  other arithmetic  90.6 us (7%)
  starting transfers between devices  24.9 us (2%)
  between operations  15.1 us (1%)
    reduce_scatter x4, waiting for transfers between devices, sum_rows(): lax.psum_scatter(whole.astype(jnp.bfloat16), 'dp', scatter_dimension=0, t...  158 us
    all_to_all x4, waiting for transfers between devices, exchange(): return lax.all_to_all(pieces, 'tensor', 0, 0)  115 us
    dot_general x5, matrix products, _nt(): lax.dot_general(left, right, (((1,), (1,)), ((), ())), preferred_element_...  111 us
    reduce_scatter x4, waiting for transfers between devices, sum_rows(): share = lax.psum_scatter(share, 'tensor', scatter_dimension=0, tiled=True)  100 us
    pallas_call x1, Pallas kernels, attend_back(): pl.pallas_call(partial(_attend_back_kernel, width=width, rows=min(256, se...  98.1 us
    psum x1, blocking collectives, whole_latents(): lax.psum(jnp.concatenate([fc2_bias_part, proj_bias_part, fc1_bias_part, q...  78.6 us
    all_gather x1, blocking collectives, whole_latents(): qv_bias_full = lax.all_gather(qv_bias, 'tensor', axis=0).astype(jnp.float32)  71.4 us
    pallas_call x1, Pallas kernels, attend(): pl.pallas_call(partial(_attend_kernel, width=width, rows=min(256, seq)),...  70.3 us
  transfers between devices with their start and end apart: 20, of which 7 were waited for; matrix products, arithmetic and copies ran while one was open for 21% of the time, Pallas kernels for 5%

profile of v1, /device:TPU:0, one launch (start us, length us, event | category | flops | bytes accessed | tf_op | source)
XLA Modules:
  0.0 1304.3 jit_solution(7277529391988920645)
XLA Ops:
  33.4 114.9 %all-to-all-done = bf16[4,2,256,1024]{3,2,1,0:T(8,128)(2,1)} async-done(((bf16[4,2,256,1024]{3,2,1,0:T(8,128)(2,1)}), bf16[4,2,256,1024]{3,2,1,0:T(8,128)(2,1)}, u32[]{:S(2)}, u32[]{:S(2)}) %all-to-all-start) | async-done | bytes 4194336 | tf_op jit(solution)/shard_map/all_to_all | solution.py:470
  159.7 71.4 %all-gather.1 = bf16[4,2,256]{2,1,0:T(2,128)(2,1)S(1)} all-gather(bf16[1,2,256]{2,1,0:T(2,128)(2,1)S(1)} %bitcast.368), channel_id=2, replica_groups=mesh['dp'=8,'tensor'=4] {'tensor'}, dimensions={0}, use_global_device_ids=true | all-gather | bytes 5120 | tf_op jit(solution)/shard_map/all_gather | solution.py:556
  231.2 38.5 %all_gather.48 = bf16[4096]{0:T(1024)(128)(2,1)S(1)} all-gather(bf16[1024]{0:T(1024)(128)(2,1)S(1)} %copy-done.39), channel_id=1, replica_groups=mesh['dp'=8,'tensor'=4] {'tensor'}, dimensions={0}, use_global_device_ids=true | all-gather | bytes 10240 | tf_op jit(solution)/shard_map/all_gather | solution.py:554
  304.9 19.4 %add_convert_fusion.qkv_ref = bf16[2048,3072]{1,0:T(8,128)(2,1)} fusion(bf16[2048,1024]{1,0:T(8,128)(2,1)} %fusion.8, bf16[3072,1024]{1,0:T(8,128)(2,1)} %all-gather.10.cloned.1.call-done, f32[3072]{0:T(1024)S(1)} %add.211), kind=kOutput, calls=%fused_computation.10 | convolution fusion | flops 12897484800 | bytes 23080960 | tf_op jit(solution)/shard_map/dot_general | solution.py:308
  324.3 70.3 %attend.1 = (bf16[2048,1024]{1,0:T(8,128)(2,1)S(1)}, f32[2048,512]{1,0:T(8,128)S(1)}) custom-call(bf16[2048,3072]{1,0:T(8,128)(2,1)} %add_convert_fusion.qkv_ref), custom_call_target="tpu_custom_call" | custom-call | flops 34359738368 | bytes 20971520 | tf_op jit(solution)/shard_map/attend/pallas_call | solution.py:350
  422.9 35.1 %multiply_convert_fusion = (bf16[2048,4096]{1,0:T(8,128)(2,1)}, f32[2048,4096]{1,0:T(8,128)}) fusion(f32[4096]{0:T(1024)S(1)} %bitcast.365, bf16[2048,1024]{1,0:T(8,128)(2,1)} %fusion.14, bf16[4096,1024]{0,1:T(8,128)(2,1)} %all-gather.14.cloned.1.call-done), kind=kOutput, calls=%fused_computation.9 | convolution fusion | flops 17263755264 | bytes 62930944 | tf_op jit(solution)/shard_map/dot_general | solution.py:308
  458.0 47.9 %fusion.86 = (bf16[4096]{0:T(1024)(128)(2,1)}, bf16[2048,4096]{1,0:T(8,128)(2,1)}) fusion(f32[2048,4096]{1,0:T(8,128)} %get-tuple-element.137, f32[4096]{0:T(1024)S(1)} %bitcast.366, bf16[2048,1024]{1,0:T(8,128)(2,1)} %fusion.28, bf16[4096,1024]{1,0:T(8,128)(2,1)} %all-gather.16.cloned.1.call-done), kind=kOutput, calls=%fused_computation.155 | convolution fusion | flops 17364414464 | bytes 62939136 | tf_op jit(solution)/shard_map/dot_general | solution.py:308
  505.9 26.9 %fusion.45 = (f32[2048]{0:T(1024)S(1)}, f32[2048]{0:T(1024)S(1)}, f32[2048,1024]{1,0:T(8,128)}) fusion(f32[2,1024]{1,0:T(2,128)S(1)} %get-tuple-element.114, f32[2048]{0:T(1024)S(1)} %bitcast.351, f32[2048]{0:T(1024)S(1)} %bitcast.354, f32[2048,1024]{1,0:T(8,128)} %copy-done.5, f32[2,1024]{1,0:T(2,128)S(1)} %get-tuple-element.117, ...), kind=kOutput, calls=%fused_computation.73 | convolution fusion | flops 17198739456 | bytes 46186496 | tf_op jit(solution)/shard_map/dot_general | solution.py:592
  549.8 98.1 %attend_back.1 = bf16[2048,3072]{1,0:T(8,128)(2,1)} custom-call(bf16[2048,3072]{1,0:T(8,128)(2,1)} %add_convert_fusion.qkv_ref, bf16[2048,1024]{1,0:T(8,128)(2,1)S(1)} %copy-done.3, f32[2048,512]{1,0:T(8,128)} %copy-done.4, bf16[2048,1024]{1,0:T(8,128)(2,1)} %convolution_convert_fusion.2.grad_ref), custom_call_target="tpu_custom_call" | custom-call | flops 85899345920 | bytes 37748736 | tf_op jit(solution)/shard_map/attend_back/pallas_call | solution.py:445
  647.8 15.7 %copy.121 = bf16[3072,2048]{1,0:T(8,128)(2,1)} copy(bf16[3072,2048]{0,1:T(8,128)(2,1)} %bitcast.327) | data formatting | bytes 25165824 | tf_op jit(solution)/shard_map/dot_general | solution.py:614
  663.6 19.0 %fusion.44 = (f32[2048]{0:T(1024)S(1)}, f32[2048]{0:T(1024)S(1)}, f32[2048,1024]{1,0:T(8,128)S(1)}) fusion(f32[2,1024]{1,0:T(2,128)S(1)} %copy-done.17, f32[2048]{0:T(1024)S(1)} %bitcast.361, f32[2048]{0:T(1024)S(1)} %bitcast.363, bf16[4,2,256,1024]{3,2,1,0:T(8,128)(2,1)} %all-to-all-done, bf16[2048,3072]{1,0:T(8,128)(2,1)} %attend_back.1, ...), kind=kOutput, calls=%fused_computation.70 | convolution fusion | flops 12899577856 | bytes 31498240 | tf_op jit(solution)/shard_map/dot_general | solution.py:621
  682.8 34.8 %fusion.22 = (bf16[2,1024]{1,0:T(2,128)(2,1)S(1)}, bf16[2,1024]{1,0:T(2,128)(2,1)S(1)}, bf16[2,1024]{1,0:T(2,128)(2,1)S(1)}, bf16[2,1024]{1,0:T(2,128)(2,1)S(1)}...) fusion(f32[2048,1024]{1,0:T(8,128)} %get-tuple-element.134, ...), kind=kOutput, calls=%fused_computation.40 | convolution fusion | flops 17238577152 | bytes 71413760 | tf_op jit(solution)/shard_map/dot_general | solution.py:576
  717.6 17.4 %convert_bitcast_fusion.2 = bf16[8,4,96,1024]{3,2,0,1:T(8,128)(2,1)S(1)} fusion(bf16[4,8,96,2048]{3,2,1,0:T(8,128)(2,1)} %bitcast.337, bf16[2048,1024,1,1]{1,0,3,2:T(8,128)(2,1)} %bitcast.339), kind=kOutput, calls=%fused_computation.74 | convolution fusion | flops 12888047616 | bytes 23068672 | tf_op jit(solution)/shard_map/dot_general | solution.py:614
  738.5 24.3 %convolution_convert_fusion.1 = bf16[4096,1024]{1,0:T(8,128)(2,1)} fusion(bf16[2048,4096]{1,0:T(8,128)(2,1)} %get-tuple-element.140, bf16[2048,1024]{1,0:T(8,128)(2,1)} %fusion.14), kind=kOutput, calls=%fused_computation.72 | convolution fusion | flops 17184063488 | bytes 29360128 | tf_op jit(solution)/shard_map/dot_general | solution.py:590
  762.8 24.2 %convolution_convert_fusion = bf16[4096,1024]{1,0:T(8,128)(2,1)} fusion(bf16[2048,4096]{1,0:T(8,128)(2,1)} %get-tuple-element.136, bf16[2048,1024]{1,0:T(8,128)(2,1)} %fusion.28), kind=kOutput, calls=%fused_computation.71 | convolution fusion | flops 17184063488 | bytes 29360128 | tf_op jit(solution)/shard_map/dot_general | solution.py:584
  809.5 65.3 %reduce-scatter.17.cloned.1.call-done = bf16[512,1024]{1,0:T(8,128)(2,1)} async-done(((bf16[4096,1024]{1,0:T(8,128)(2,1)}), bf16[512,1024]{1,0:T(8,128)(2,1)}) %reduce-scatter.17.cloned.1.call-update) | async-done | bytes 1048592 | tf_op jit(solution)/shard_map/reduce_scatter | solution.py:486
  874.9 20.5 %fusion.50 = (bf16[4,2,256,1024]{3,2,0,1:T(8,128)(2,1)}, bf16[4,2,256,1024]{3,2,0,1:T(8,128)(2,1)S(1)}) fusion(f32[2,4,256]{2,1,0:T(4,128)S(1)} %div.68, f32[2,4,256]{2,1,0:T(4,128)S(1)} %copy-done.21, f32[2,4,256]{2,1,0:T(4,128)S(1)} %div.66, f32[2,4,256,1024]{3,2,1,0:T(8,128)} %bitcast.329, f32[2,1024]{1,0:T(2,128)S(1)} %copy-done.17, ...), kind=kLoop, calls=%fused_computation.82 | loop fusion | flops 50331648 | bytes 50429952 | tf_op jit(solution)/shard_map/transpose | solution.py:524
  902.8 46.8 %reduce-scatter.21.cloned.1.call-done = bf16[512,1024]{1,0:T(8,128)(2,1)} async-done(((bf16[4096,1024]{1,0:T(8,128)(2,1)}), bf16[512,1024]{1,0:T(8,128)(2,1)}) %reduce-scatter.21.cloned.1.call-update) | async-done | bytes 1048592 | tf_op jit(solution)/shard_map/reduce_scatter | solution.py:486
  949.7 45.4 %reduce-scatter.13.cloned.1.call-done = bf16[128,1024]{1,0:T(8,128)(2,1)} async-done(((bf16[1024,1024]{1,0:T(8,128)(2,1)}), bf16[128,1024]{1,0:T(8,128)(2,1)}) %reduce-scatter.13.cloned.1.call-update) | async-done | bytes 262160 | tf_op jit(solution)/shard_map/reduce_scatter | solution.py:486
  995.1 25.5 %reduce-scatter.11.cloned.1.call-done = bf16[96,1024]{1,0:T(8,128)(2,1)} async-done(((bf16[384,1024]{1,0:T(8,128)(2,1)}), bf16[96,1024]{1,0:T(8,128)(2,1)}) %reduce-scatter.11.cloned.1.call-update) | async-done | bytes 196624 | tf_op jit(solution)/shard_map/reduce_scatter | solution.py:489
  1020.7 28.5 %reduce-scatter.19.cloned.1.call-done = bf16[128,1024]{1,0:T(8,128)(2,1)} async-done(((bf16[512,1024]{1,0:T(8,128)(2,1)}), bf16[128,1024]{1,0:T(8,128)(2,1)}) %reduce-scatter.19.cloned.1.call-update) | async-done | bytes 262160 | tf_op jit(solution)/shard_map/reduce_scatter | solution.py:489
  1058.9 46.0 %reduce-scatter.23.cloned.1.call-done = bf16[128,1024]{1,0:T(8,128)(2,1)} async-done(((bf16[512,1024]{1,0:T(8,128)(2,1)}), bf16[128,1024]{1,0:T(8,128)(2,1)}) %reduce-scatter.23.cloned.1.call-update) | async-done | bytes 262160 | tf_op jit(solution)/shard_map/reduce_scatter | solution.py:489
  1123.7 78.6 %psum.15 = bf16[9216]{0:T(1024)(128)(2,1)S(1)} all-reduce(bf16[9216]{0:T(1024)(128)(2,1)S(1)} %pad_maximum_fusion), channel_id=1, replica_groups=mesh['dp'=8,'tensor'=4] {'dp','tensor'}, use_global_device_ids=true, to_apply=%region_21.22 | all-reduce | flops 9216 | bytes 36864 | tf_op jit(solution)/shard_map/psum | solution.py:648
  1229.3 17.7 %psum.14 = bf16[8,1024]{1,0:T(8,128)(2,1)S(1)} all-reduce(bf16[8,1024]{1,0:T(8,128)(2,1)S(1)} %convolution_convert_fusion.3), channel_id=1, replica_groups=mesh['dp'=8,'tensor'=4] {'tensor'}, use_global_device_ids=true, to_apply=%region_14.15 | all-reduce | flops 8192 | bytes 32768 | tf_op jit(solution)/shard_map/psum | solution.py:643
  (231 shorter events, 257.0 us)
Async XLA Ops:
  7.2 297.7 %all-gather.10.cloned.1.call-start = ((), (), s32[]{:S(2)}) async-start(), calls=%async_computation.13 | async-start | bytes 6488064 | tf_op jit(solution)/shard_map/all_gather | solution.py:476
  11.6 387.0 %all-gather.12.cloned.1.call-start = ((), (), s32[]{:S(2)}) async-start(), calls=%async_computation.14 | async-start | bytes 2162688 | tf_op jit(solution)/shard_map/all_gather | solution.py:476
  13.2 409.7 %all-gather.14.cloned.1.call-start = ((), (), s32[]{:S(2)}) async-start(), calls=%async_computation.15 | async-start | bytes 8650752 | tf_op jit(solution)/shard_map/all_gather | solution.py:476
  20.5 127.7 %all-to-all-start = ((bf16[4,2,256,1024]{3,2,1,0:T(8,128)(2,1)}), bf16[4,2,256,1024]{3,2,1,0:T(8,128)(2,1)}, u32[]{:S(2)}, u32[]{:S(2)}) async-start(bf16[4,2,256,1024]{3,2,1,0:T(8,128)(2,1)} %bitcast.336), calls=%async_computation | async-start | bytes 8388608 | tf_op jit(solution)/shard_map/all_to_all | solution.py:470
  33.4 197.8 %copy-start.38 = (bf16[1024]{0:T(1024)(128)(2,1)S(1)}, bf16[1024]{0:T(1024)(128)(2,1)}, u32[]{:S(2)}) copy-start(bf16[1024]{0:T(1024)(128)(2,1)} %param.19) | copy-start | bytes 6148
  33.4 197.8 %copy-start.39 = (bf16[1024]{0:T(1024)(128)(2,1)S(1)}, bf16[1024]{0:T(1024)(128)(2,1)}, u32[]{:S(2)}) copy-start(bf16[1024]{0:T(1024)(128)(2,1)} %param.21) | copy-start | bytes 6148
  33.4 236.3 %copy-start.40 = (bf16[1024]{0:T(1024)(128)(2,1)S(1)}, bf16[1024]{0:T(1024)(128)(2,1)}, u32[]{:S(2)}) copy-start(bf16[1024]{0:T(1024)(128)(2,1)} %param.23) | copy-start | bytes 6148
  33.4 236.9 %copy-start.8 = (bf16[8,1024]{1,0:T(8,128)(2,1)S(1)}, bf16[8,1024]{1,0:T(8,128)(2,1)}, u32[]{:S(2)}) copy-start(bf16[8,1024]{1,0:T(8,128)(2,1)} %param.14) | copy-start | bytes 49156
  148.3 146.5 %all-to-all-start.2 = ((bf16[4,2,256,1024]{3,2,1,0:T(8,128)(2,1)}), bf16[4,2,256,1024]{3,2,1,0:T(8,128)(2,1)}, u32[]{:S(2)}, u32[]{:S(2)}) async-start(bf16[4,2,256,1024]{3,2,1,0:T(8,128)(2,1)} %bitcast.335), calls=%async_computation.2 | async-start | bytes 8388608 | tf_op jit(solution)/shard_map/all_to_all | solution.py:470
  153.1 304.9 %all-gather.16.cloned.1.call-start = ((), (), s32[]{:S(2)}) async-start(), calls=%async_computation.16 | async-start | bytes 8650752 | tf_op jit(solution)/shard_map/all_gather | solution.py:476
  154.9 648.5 %reduce-scatter.9.cloned.1.call-start = ((), (), s32[]{:S(2)}) async-start(), calls=%async_computation.17 | async-start | bytes 7077888 | tf_op jit(solution)/shard_map/reduce_scatter | solution.py:486
  738.4 136.4 %reduce-scatter.17.cloned.1.call-start = ((), (), s32[]{:S(2)}) async-start(), calls=%async_computation.22 | async-start | bytes 9437184 | tf_op jit(solution)/shard_map/reduce_scatter | solution.py:486
  762.8 186.8 %reduce-scatter.21.cloned.1.call-start = ((), (), s32[]{:S(2)}) async-start(), calls=%async_computation.25 | async-start | bytes 9437184 | tf_op jit(solution)/shard_map/reduce_scatter | solution.py:486
  787.0 208.0 %reduce-scatter.13.cloned.1.call-start = ((), (), s32[]{:S(2)}) async-start(), calls=%async_computation.20 | async-start | bytes 2359296 | tf_op jit(solution)/shard_map/reduce_scatter | solution.py:486
  803.3 217.3 %reduce-scatter.11.cloned.1.call-start = ((), (), s32[]{:S(2)}) async-start(), calls=%async_computation.18 | async-start | bytes 983040 | tf_op jit(solution)/shard_map/reduce_scatter | solution.py:489
  806.1 91.7 %all-to-all-start.4 = ((bf16[4,2,1536]{2,1,0:T(2,128)(2,1)}), bf16[4,2,1536]{2,1,0:T(2,128)(2,1)S(1)}, u32[]{:S(2)}, u32[]{:S(2)}) async-start(bf16[4,2,1536]{2,1,0:T(2,128)(2,1)} %reshape.438), calls=%async_computation.4 | async-start | bytes 49152 | tf_op jit(solution)/shard_map/all_to_all | solution.py:633
  809.5 239.8 %reduce-scatter.19.cloned.1.call-start = ((), (), s32[]{:S(2)}) async-start(), calls=%async_computation.23 | async-start | bytes 1310720 | tf_op jit(solution)/shard_map/reduce_scatter | solution.py:489
  897.8 156.1 %all-to-all-start.1 = ((bf16[4,2,256,1024]{3,2,1,0:T(8,128)(2,1)}), bf16[4,2,256,1024]{3,2,1,0:T(8,128)(2,1)}, u32[]{:S(2)}, u32[]{:S(2)}) async-start(bf16[4,2,256,1024]{3,2,1,0:T(8,128)(2,1)} %copy.114), calls=%async_computation.1 | async-start | bytes 8388608 | tf_op jit(solution)/shard_map/all_to_all | solution.py:470
  902.7 202.2 %reduce-scatter.23.cloned.1.call-start = ((), (), s32[]{:S(2)}) async-start(), calls=%async_computation.26 | async-start | bytes 1310720 | tf_op jit(solution)/shard_map/reduce_scatter | solution.py:489
  949.6 298.0 %reduce-scatter.15.cloned.1.call-start = ((), (), s32[]{:S(2)}) async-start(), calls=%async_computation.21 | async-start | bytes 327680 | tf_op jit(solution)/shard_map/reduce_scatter | solution.py:489
  995.1 281.6 %all-gather.18.cloned.1.call-start = ((), (), s32[]{:S(2)}) async-start(), calls=%async_computation.19 | async-start | bytes 1769472 | tf_op jit(solution)/shard_map/all_gather | solution.py:490
  1020.7 263.0 %all-gather.20.cloned.1.call-start = ((), (), s32[]{:S(2)}) async-start(), calls=%async_computation.24 | async-start | bytes 2359296 | tf_op jit(solution)/shard_map/all_gather | solution.py:490
  1053.9 211.3 %all-to-all-start.3 = ((bf16[4,2,256,1024]{3,2,1,0:T(8,128)(2,1)}), bf16[4,2,256,1024]{3,2,1,0:T(8,128)(2,1)}, u32[]{:S(2)}, u32[]{:S(2)}) async-start(bf16[4,2,256,1024]{3,2,1,0:T(8,128)(2,1)} %copy.117), calls=%async_computation.3 | async-start | bytes 8388608 | tf_op jit(solution)/shard_map/all_to_all | solution.py:470
  1058.8 234.4 %all-gather.22.cloned.1.call-start = ((), (), s32[]{:S(2)}) async-start(), calls=%async_computation.27 | async-start | bytes 2359296 | tf_op jit(solution)/shard_map/all_gather | solution.py:490
  (39 other events, 1079.0 us)
Sparse Core Ops, SparseCore 0:
  11.7 136.6 all-gather.9
  151.9 101.2 all-gather.11
  256.6 94.8 all-gather.13
  354.8 75.7 all-gather.15
  738.5 61.2 reduce-scatter.8
  803.5 71.2 reduce-scatter.16
  878.3 71.2 reduce-scatter.20
  953.8 41.2 reduce-scatter.12
  997.4 23.2 reduce-scatter.10
  1022.8 26.4 reduce-scatter.18
  1051.7 53.1 reduce-scatter.22
  1107.0 58.5 reduce-scatter.14
  1167.6 25.3 all-gather.17
  1194.9 27.8 all-gather.19
  1224.8 27.8 all-gather.21

commit v2 on v1

--- a/solution.py
+++ b/solution.py
@@ -463,31 +463,152 @@
     )(qkv, out, lse, grad)
 
 
-BY_OWNER, BY_SHARE = ("tensor", "dp"), ("dp", "tensor")
-
-
-def exchange(pieces):
-    return lax.all_to_all(pieces, "tensor", 0, 0)
-
-
-def gather_rows(part, order):
-    share = part.shape[0] // lax.axis_size("dp")
-    mine = lax.dynamic_slice_in_dim(part, lax.axis_index("dp") * share, share, 0)
-    return lax.all_gather(mine, order, axis=0, tiled=True)
-
-
-def by_share(rows):
-    groups, shares = lax.axis_size("tensor"), lax.axis_size("dp")
-    split = rows.reshape(groups, shares, -1, *rows.shape[1:])
-    return jnp.swapaxes(split, 0, 1).reshape(rows.shape)
-
-
-def sum_rows(whole):
-    share = lax.psum_scatter(
-        whole.astype(jnp.bfloat16), "dp", scatter_dimension=0, tiled=True
-    )
-    share = lax.psum_scatter(share, "tensor", scatter_dimension=0, tiled=True)
-    return lax.all_gather(share, "dp", axis=0, tiled=True).astype(jnp.float32)
+SHARES, GROUPS = 8, 4
+
+
+def xor_permute(array, axis, mask):
+    size = lax.axis_size(axis)
+    return lax.ppermute(array, axis, [(index, index ^ mask) for index in range(size)])
+
+
+def xor_order(array, index, axes):
+    for place, axis in enumerate(reversed(axes)):
+        array = jnp.where((index >> place) & 1 == 1, jnp.flip(array, axis), array)
+    return array
+
+
+def add_low(left, right):
+    return (left.astype(jnp.float32) + right.astype(jnp.float32)).astype(jnp.bfloat16)
+
+
+def _merge_kernel(*refs):
+    *piece_refs, array_ref = refs
+    pieces = [ref[member] for member in range(GROUPS) for ref in piece_refs]
+    array_ref[...] = jnp.swapaxes(
+        jnp.stack([piece.astype(jnp.float32) for piece in pieces], 0), 0, 1
+    ).astype(array_ref.dtype)
+
+
+def merge_latents(pieces, dtype):
+    _, count, depth = pieces[0].shape
+    step, latents = 32, len(pieces)
+    size = GROUPS * latents * count * depth
+    return pl.pallas_call(
+        _merge_kernel,
+        grid=(count // step,),
+        in_specs=[pl.BlockSpec((GROUPS, step, depth), lambda i: (0, i, 0))] * latents,
+        out_specs=pl.BlockSpec((step, GROUPS * latents, depth), lambda i: (i, 0, 0)),
+        out_shape=jax.ShapeDtypeStruct((count, GROUPS * latents, depth), dtype),
+        cost_estimate=pl.CostEstimate(flops=0, bytes_accessed=6 * size, transcendentals=0),
+        name="merge_latents",
+    )(*pieces)
+
+
+class Flow:
+    def __init__(self, stages):
+        self.stages, self.result = stages, None
+        self.values = next(stages)
+
+    def advance(self, values):
+        try:
+            self.values = self.stages.send(values)
+        except StopIteration as stop:
+            self.values, self.result = (), stop.value
+
+
+def window(compute, *flows):
+    compute, values = lax.optimization_barrier((compute, [flow.values for flow in flows]))
+    for flow, value in zip(flows, values):
+        flow.advance(value)
+    return compute
+
+
+def sent(array, move):
+    array = yield move(array)
+    return array
+
+
+def gather_local(mine, shares, pauses):
+    place = lax.axis_index("dp")
+    near, far = xor_permute(mine, "tensor", 1), xor_permute(mine, "tensor", 2)
+    got = (near, far, xor_permute(far, "tensor", 1))
+    if 0 in pauses:
+        got = yield got
+    block = jnp.stack(got, 0)
+    half = mine.shape[0] // 2
+    along_x, along_y = xor_permute(block, "dp", 2), xor_permute(block, "dp", 4)
+    other = xor_permute(block, "dp", 1)
+    if 1 in pauses:
+        block, along_x, along_y, other = yield (block, along_x, along_y, other)
+    halves = [xor_permute(along_x[:, :half], "dp", 4), xor_permute(along_y[:, half:], "dp", 2)]
+    others = [other, xor_permute(along_x, "dp", 1), xor_permute(along_y, "dp", 1)]
+    if 2 in pauses:
+        halves, others = yield (halves, others)
+    across = jnp.concatenate(halves, 1)
+    chips = [block, along_x, along_y, across]
+    blocks = yield [chips, [*others, xor_permute(across, "dp", 1)]]
+    return [
+        [
+            jnp.concatenate(
+                [
+                    lax.dynamic_index_in_dim(shares, place ^ (2 * chip + core), 0),
+                    blocks[core][chip],
+                ],
+                0,
+            )
+            for chip in range(4)
+        ]
+        for core in range(2)
+    ]
+
+
+def reduce_local(blocks, pauses):
+    half = blocks.shape[3] // 2
+    pair = (blocks[0], xor_permute(blocks[1], "dp", 1))
+    if 0 in pauses:
+        pair = yield pair
+    total = add_low(*pair)
+    total = total.reshape(2, 2, *total.shape[1:])
+    first, second = total[:, :, :, :half], total[:, :, :, half:]
+    pairs = (
+        (first[:, 0], xor_permute(first[:, 1], "dp", 2)),
+        (second[0], xor_permute(second[1], "dp", 4)),
+    )
+    if 1 in pauses:
+        pairs = yield pairs
+    first, second = [add_low(*pair) for pair in pairs]
+    pairs = (
+        (first[0], xor_permute(first[1], "dp", 4)),
+        (second[0], xor_permute(second[1], "dp", 2)),
+    )
+    if 2 in pauses:
+        pairs = yield pairs
+    total = jnp.concatenate([add_low(*pair) for pair in pairs], 1)
+    total = total.reshape(2, 2, *total.shape[1:])
+    total = add_low(total[:, 0], xor_permute(total[:, 1], "tensor", 1))
+    pair = (total[0], xor_permute(total[1], "tensor", 2))
+    pair = yield pair
+    return add_low(*pair)
+
+
+def gathered(*shares):
+    sizes = [share.shape[0] for share in shares]
+    share = jnp.concatenate(shares, 0) if len(shares) > 1 else shares[0]
+    whole = yield lax.all_gather(share, "dp", axis=0)
+    parts, at = [], 0
+    for size in sizes:
+        parts.append(whole[:, at : at + size])
+        at += size
+    return parts
+
+
+def group_send(pieces):
+    return [pieces[0]] + [xor_permute(pieces[mask], "tensor", mask) for mask in range(1, GROUPS)]
+
+
+def group_add(pieces):
+    first, second, third, fourth = [piece.astype(jnp.float32) for piece in pieces]
+    return (first + second) + (third + fourth)
 
 
 def whole_latents(
@@ -506,27 +627,54 @@
     ada_bias,
 ):
     row_count, group_latents, model_width = tokens.shape
-    groups = lax.axis_size("tensor")
-    latents = group_latents // groups
-    seq = row_count * groups
+    latents = group_latents // GROUPS
+    seq = row_count * GROUPS
     width = qkv_weight.shape[2]
     hidden = fc1_weight.shape[1]
     rows = latents * seq
-    me = lax.axis_index("tensor")
-
-    def to_latents(array):
+    part, slot = hidden // SHARES, width // SHARES
+    me, place = lax.axis_index("tensor"), lax.axis_index("dp")
+
+    def split_tokens(array):
         pieces = jnp.transpose(
-            array.reshape(row_count, groups, latents, model_width), (1, 2, 0, 3)
+            array.reshape(row_count, GROUPS, latents, model_width), (1, 2, 0, 3)
         )
-        return jnp.transpose(exchange(pieces), (1, 0, 2, 3)).reshape(latents, seq, model_width)
-
-    def to_tokens(array):
-        pieces = jnp.transpose(
-            array.reshape(latents, groups, row_count, model_width), (1, 0, 2, 3)
+        return [pieces[:, index] for index in range(latents)]
+
+    def exchange(pieces):
+        return lax.all_to_all(pieces, "tensor", 0, 0)
+
+    def contract(left, right):
+        return lax.dot_general(
+            left, right, (((0,), (0,)), ((), ())), preferred_element_type=jnp.float32
         )
-        return jnp.transpose(exchange(pieces), (2, 0, 1, 3)).reshape(
-            row_count, group_latents, model_width
-        )
+
+    qkv_t = jnp.transpose(qkv_weight.reshape(model_width, 3, SHARES, slot), (2, 1, 3, 0))
+    attention_shares = jnp.concatenate(
+        [
+            qkv_t.reshape(SHARES, 3 * slot, model_width),
+            output_projection_weight.reshape(SHARES, slot, model_width),
+        ],
+        1,
+    )
+    own_qkv = lax.dynamic_index_in_dim(
+        qkv_weight.reshape(model_width, 3, SHARES, slot), place, 2, keepdims=False
+    )
+    own_attention = jnp.concatenate(
+        [
+            jnp.transpose(own_qkv, (1, 2, 0)).reshape(3 * slot, model_width),
+            lax.dynamic_slice_in_dim(output_projection_weight, place * slot, slot, 0),
+        ],
+        0,
+    )
+    weights = Flow(gather_local(own_attention, attention_shares, (0,)))
+    pieces = window(split_tokens(tokens), weights)
+    incoming = [Flow(sent(pieces[0], exchange))]
+    grad_pieces = split_tokens(cotangent)
+    fc1_shares = fc1_weight.T.reshape(SHARES, part, model_width)
+    fc2_shares = fc2_weight.reshape(SHARES, part, model_width)
+    own_fc1 = lax.dynamic_index_in_dim(fc1_shares, place, 0, keepdims=False)
+    own_fc2 = lax.dynamic_index_in_dim(fc2_shares, place, 0, keepdims=False)
 
     cond_float = cond.astype(jnp.float32)
     silu_c = jax.nn.silu(cond_float).astype(jnp.bfloat16)
@@ -534,136 +682,281 @@
     mod_part = jnp.dot(silu_c, ada_flat, preferred_element_type=jnp.float32) + ada_bias.reshape(
         6 * width
     ).astype(jnp.float32)
-    mod_part = mod_part.reshape(group_latents, 6, width).astype(jnp.bfloat16)
-    modulation = lax.dynamic_slice_in_dim(
-        lax.all_gather(mod_part, "tensor", axis=2, tiled=True), me * latents, latents, 0
+    mod_part = mod_part.astype(jnp.bfloat16).reshape(GROUPS, latents, 6, width)
+    mod_got = []
+    for mask in range(GROUPS):
+        piece = lax.dynamic_index_in_dim(mod_part, me ^ mask, 0, keepdims=False)
+        mod_got.append(xor_permute(piece, "tensor", mask) if mask else piece)
+    modulation = xor_order(jnp.stack(mod_got, 0).reshape(2, 2, latents, 6, width), me, (0, 1))
+    modulation = jnp.transpose(
+        modulation.reshape(GROUPS, latents, 6, width), (1, 2, 0, 3)
+    ).reshape(latents, 6, model_width)
+    own_biases = jnp.concatenate([fc1_bias, qv_bias.reshape(2 * width)])
+    bias_all = jnp.stack(
+        [own_biases] + [xor_permute(own_biases, "tensor", mask) for mask in range(1, GROUPS)], 0
     ).astype(jnp.float32)
+    fc1_bias_all = jnp.transpose(
+        xor_order(bias_all[:, :hidden].reshape(GROUPS, 2, 2, 2, part), place, (1, 2, 3)),
+        (3, 1, 2, 0, 4),
+    ).reshape(GROUPS * hidden)
+    qv_all = xor_order(
+        bias_all[:, hidden:].reshape(GROUPS, 2, 2, 2, 2, slot), place, (2, 3, 4)
+    ).reshape(GROUPS, 2, width)
+    qkv_bias = jnp.stack([qv_all[:, 0], jnp.zeros_like(qv_all[:, 0]), qv_all[:, 1]], 1).reshape(
+        GROUPS * 3 * width
+    )
+
+    modulation, attention_shares = window((modulation, attention_shares), weights)
+    attention_all = jnp.stack([jnp.stack(chips, 0) for chips in weights.result], 0)
+    qkv_rows = jnp.transpose(
+        attention_all[:, :, :, : 3 * slot].reshape(2, 4, GROUPS, 3, slot, model_width),
+        (2, 3, 1, 0, 4, 5),
+    ).reshape(GROUPS * 3 * width, model_width)
+    proj_rows = jnp.transpose(attention_all[:, :, :, 3 * slot :], (2, 1, 0, 3, 4)).reshape(
+        GROUPS * width, model_width
+    )
+    (modulation, qkv_rows, proj_rows, pieces, grad_pieces, fc1_shares, own_fc1, own_fc2) = window(
+        (modulation, qkv_rows, proj_rows, pieces, grad_pieces, fc1_shares, own_fc1, own_fc2),
+        incoming[0],
+    )
+    modulation = modulation.astype(jnp.float32)
     shift1, scale1, gate1, shift2, scale2, gate2 = [
         modulation[:, index][:, None] for index in range(6)
     ]
-
-    qkv_rows = gather_rows(
-        jnp.transpose(qkv_weight, (1, 2, 0)).reshape(3 * width, model_width),
-        BY_OWNER,
-    )
-    inputs_float = to_latents(tokens).astype(jnp.float32)
-    proj_rows = gather_rows(output_projection_weight, BY_OWNER)
-    fc1_rows = gather_rows(fc1_weight.T, BY_SHARE)
-    fc2_rows = gather_rows(fc2_weight, BY_SHARE)
-    fc1_bias_full = by_share(
-        lax.all_gather(fc1_bias, "tensor", axis=0, tiled=True)
-    ).astype(jnp.float32)
-    qv_bias_full = lax.all_gather(qv_bias, "tensor", axis=0).astype(jnp.float32)
-    qkv_bias = jnp.stack(
-        [qv_bias_full[:, 0], jnp.zeros_like(qv_bias_full[:, 0]), qv_bias_full[:, 1]], 1
-    ).reshape(groups * 3 * width)
-    grad_out = to_latents(cotangent).astype(jnp.float32)
-
-    norm1, inverse1 = layer_stats(inputs_float)
-    attn_in = (norm1 * (1.0 + scale1) + shift1).astype(jnp.bfloat16).reshape(rows, model_width)
-    qkv = (_nt(attn_in, qkv_rows) + qkv_bias).astype(jnp.bfloat16)
-    attended, log_totals = attend(qkv, latents, groups, width, seq)
+    fc1_flow = Flow(gather_local(own_fc1, fc1_shares, (0, 1, 2)))
+    tokens_in, attn_in, qkv, attended, log_totals = [], [], [], [], []
+    for index in range(latents):
+        tokens_in.append(incoming[index].result.reshape(seq, model_width))
+        normed = layer_stats(tokens_in[index].astype(jnp.float32))[0]
+        attn_in.append((normed * (1.0 + scale1[index]) + shift1[index]).astype(jnp.bfloat16))
+        qkv.append((_nt(attn_in[index], qkv_rows) + qkv_bias).astype(jnp.bfloat16))
+        if index == 0:
+            qkv[0], pieces = window((qkv[0], pieces), fc1_flow)
+            incoming += [Flow(sent(pieces[other], exchange)) for other in range(1, latents)]
+        if index == 1:
+            qkv[1], grad_pieces = window((qkv[1], grad_pieces), fc1_flow, fc2_flow)
+            grad_flows = [Flow(sent(grad_pieces[0], exchange))]
+        result, totals = attend(qkv[index], 1, GROUPS, width, seq)
+        if index == 0:
+            result, own_fc2 = window((result, own_fc2), fc1_flow, *incoming[1:])
+            fc2_flow = Flow(gather_local(own_fc2, fc2_shares, (0, 1, 2)))
+        if index == 1:
+            result, grad_pieces = window((result, grad_pieces), fc1_flow, fc2_flow, *grad_flows)
+            grad_flows += [
+                Flow(sent(grad_pieces[other], exchange)) for other in range(1, latents)
+            ]
+        attended.append(result)
+        log_totals.append(totals)
+
+    def dense(blocks):
+        return jnp.concatenate(
+            [block.reshape(-1, model_width) for chips in blocks for block in chips], 0
+        )
+
+    fc1_rows = dense(fc1_flow.result)
+    attended_all = jnp.concatenate(attended, 0)
+    inputs_float = jnp.stack(tokens_in, 0).astype(jnp.float32)
     attn_out = (
-        jnp.dot(attended, proj_rows, preferred_element_type=jnp.float32)
+        jnp.dot(attended_all, proj_rows, preferred_element_type=jnp.float32)
         + proj_bias.astype(jnp.float32)
     ).reshape(latents, seq, model_width)
+
+    attn_out = window(attn_out, fc2_flow)
     mid = inputs_float + gate1 * attn_out
     norm2, inverse2 = layer_stats(mid)
     mlp_in = (norm2 * (1.0 + scale2) + shift2).astype(jnp.bfloat16).reshape(rows, model_width)
-    pre = _nt(mlp_in, fc1_rows) + fc1_bias_full
+    pre = _nt(mlp_in, fc1_rows) + fc1_bias_all
     act = jax.nn.gelu(pre, approximate=True).astype(jnp.bfloat16)
+    act, pre = window((act, pre), fc2_flow, *grad_flows[1:])
+    fc2_rows = dense(fc2_flow.result)
+    grad_out = jnp.stack(
+        [flow.result.reshape(seq, model_width) for flow in grad_flows], 0
+    ).astype(jnp.float32)
     mlp_out = (
         jnp.dot(act, fc2_rows, preferred_element_type=jnp.float32) + fc2_bias.astype(jnp.float32)
     ).reshape(latents, seq, model_width)
-    output = to_tokens((mid + gate2 * mlp_out).astype(jnp.bfloat16))
-
+    out_local = (mid + gate2 * mlp_out).astype(jnp.bfloat16)
     grad_gate2 = jnp.sum(grad_out * mlp_out, 1)
     d_mlp = (grad_out * gate2).astype(jnp.bfloat16).reshape(rows, model_width)
+    out_local, grad_gate2, d_mlp = lax.optimization_barrier((out_local, grad_gate2, d_mlp))
+    out_pieces = jnp.transpose(
+        out_local.reshape(latents, GROUPS, row_count, model_width), (1, 0, 2, 3)
+    )
+    out_flow = Flow(sent(out_pieces, exchange))
+    dense_shape = (2, 4, GROUPS, part, model_width)
     fc2_bias_part = jnp.sum(d_mlp.astype(jnp.float32), 0)
-    grad_fc2 = sum_rows(
-        lax.dot_general(act, d_mlp, (((0,), (0,)), ((), ())), preferred_element_type=jnp.float32)
-    )
+    fc2_local = contract(act, d_mlp).astype(jnp.bfloat16)
+    d_mlp, fc2_local = lax.optimization_barrier((d_mlp, fc2_local))
+    fc2_sum = Flow(reduce_local(fc2_local.reshape(dense_shape), (0, 1, 2)))
     d_act = _nt(d_mlp, fc2_rows)
     d_pre = jax.vjp(partial(jax.nn.gelu, approximate=True), pre)[1](d_act)[0].astype(jnp.bfloat16)
+    d_pre = window(d_pre, fc2_sum)
     fc1_bias_part = jnp.sum(d_pre.astype(jnp.float32), 0)
-    grad_fc1 = sum_rows(
-        lax.dot_general(d_pre, mlp_in, (((0,), (0,)), ((), ())), preferred_element_type=jnp.float32)
-    ).T
+    fc1_local = contract(d_pre, mlp_in).astype(jnp.bfloat16)
+    d_pre, fc1_local = window((d_pre, fc1_local), fc2_sum, out_flow)
+    fc1_sum = Flow(reduce_local(fc1_local.reshape(dense_shape), (0, 1, 2)))
     d_mlp_in = jnp.dot(d_pre, fc1_rows, preferred_element_type=jnp.float32).reshape(
         latents, seq, model_width
     )
+    d_mlp_in = window(d_mlp_in, fc2_sum, fc1_sum)
     grad_shift2 = jnp.sum(d_mlp_in, 1)
     grad_scale2 = jnp.sum(d_mlp_in * norm2, 1)
     d_mid = grad_out + norm_back(d_mlp_in * (1.0 + scale2), norm2, inverse2)
     grad_gate1 = jnp.sum(d_mid * attn_out, 1)
     d_attn = (d_mid * gate1).astype(jnp.bfloat16).reshape(rows, model_width)
     proj_bias_part = jnp.sum(d_attn.astype(jnp.float32), 0)
-    grad_proj = sum_rows(
-        by_share(
-            lax.dot_general(
-                attended, d_attn, (((0,), (0,)), ((), ())), preferred_element_type=jnp.float32
+    proj_local = contract(attended_all, d_attn).astype(jnp.bfloat16)
+    d_attended = _nt(d_attn, proj_rows).astype(jnp.bfloat16)
+    d_attended, proj_local = window((d_attended, proj_local), fc2_sum, fc1_sum)
+    fc2_rows_flow = Flow(gathered(fc2_sum.result))
+    proj_sum = Flow(
+        reduce_local(
+            jnp.transpose(proj_local.reshape(GROUPS, 4, 2, slot, model_width), (2, 1, 0, 3, 4)),
+            (1,),
+        )
+    )
+
+    fc1_true = xor_order(
+        jnp.transpose(fc1_bias_part.reshape(2, 2, 2, GROUPS, part), (3, 1, 2, 0, 4)),
+        place,
+        (1, 2, 3),
+    ).reshape(GROUPS, hidden)
+    everywhere = jnp.concatenate([fc2_bias_part, proj_bias_part])
+
+    def sum_biases():
+        own = [
+            jnp.concatenate([fc1_true[mask], everywhere]).astype(jnp.bfloat16)
+            for mask in range(GROUPS)
+        ]
+        total = yield group_send(own)
+        total = group_add(total).astype(jnp.bfloat16)
+        pair = yield (total, xor_permute(total, "dp", 1))
+        total = add_low(*pair)
+        total = add_low(total, xor_permute(total, "dp", 2))
+        pair = yield (total, xor_permute(total, "dp", 4))
+        return add_low(*pair).astype(jnp.float32)
+
+    biases = Flow(sum_biases())
+
+    d_qkv, grad_shift1, grad_scale1, returned = [], [], [], []
+    d_attended = [d_attended[index * seq : (index + 1) * seq] for index in range(latents)]
+    qkv_local, qkv_bias_part = 0.0, 0.0
+    qkv_sum = None
+    for index in range(latents):
+        d_qkv.append(
+            attend_back(
+                qkv[index],
+                attended[index],
+                log_totals[index],
+                d_attended[index],
+                1,
+                GROUPS,
+                width,
+                seq,
             )
         )
-    )
-    d_attended = _nt(d_attn, proj_rows).astype(jnp.bfloat16)
-    d_qkv = attend_back(qkv, attended, log_totals, d_attended, latents, groups, width, seq)
-    qkv_bias_part = jnp.sum(d_qkv.astype(jnp.float32), 0)
+        last = index == latents - 1
+        if index == 0:
+            d_qkv[0] = window(d_qkv[0], fc2_rows_flow, fc1_sum, proj_sum, biases)
+        if last:
+            d_qkv[index] = window(d_qkv[index], later_rows_flow, biases, *returned)
+        qkv_bias_part = qkv_bias_part + jnp.sum(d_qkv[index].astype(jnp.float32), 0)
+        qkv_local = qkv_local + contract(d_qkv[index], attn_in[index])
+        if last:
+            qkv_blocks = jnp.transpose(
+                qkv_local.astype(jnp.bfloat16).reshape(GROUPS, 3, 4, 2, slot, model_width),
+                (3, 2, 0, 1, 4, 5),
+            ).reshape(2, 4, GROUPS, 3 * slot, model_width)
+            d_qkv[index], qkv_blocks = lax.optimization_barrier((d_qkv[index], qkv_blocks))
+            qkv_sum = Flow(reduce_local(qkv_blocks, (0,)))
+        d_attn_in = jnp.dot(d_qkv[index], qkv_rows, preferred_element_type=jnp.float32)
+        norm1, inverse1 = layer_stats(tokens_in[index].astype(jnp.float32))
+        grad_shift1.append(jnp.sum(d_attn_in, 0))
+        grad_scale1.append(jnp.sum(d_attn_in * norm1, 0))
+        local = d_mid[index] + norm_back(d_attn_in * (1.0 + scale1[index]), norm1, inverse1)
+        local = local.astype(jnp.bfloat16).reshape(GROUPS, row_count, model_width)
+        if last:
+            local = window(local, qkv_sum)
+        else:
+            flows = (fc1_sum, proj_sum, biases)
+            (local, d_attended[index + 1], qkv_local) = window(
+                (local, d_attended[index + 1], qkv_local), *(flows if index == 0 else ())
+            )
+        returned.append(Flow(sent(local, exchange)))
+        if index == 0:
+            later_rows_flow = Flow(gathered(fc1_sum.result, proj_sum.result))
+    window((), qkv_sum, returned[-1])
+    qkv_rows_flow = Flow(gathered(qkv_sum.result))
+    qkv_rows_flow.advance(qkv_rows_flow.values)
+    grad_tokens = merge_latents([flow.result for flow in returned], jnp.float32)
+    output = jnp.transpose(out_flow.result, (2, 0, 1, 3)).reshape(
+        row_count, group_latents, model_width
+    )
+    grad_fc2 = fc2_rows_flow.result[0].reshape(hidden, model_width).astype(jnp.float32)
+    grad_fc1 = later_rows_flow.result[0].reshape(hidden, model_width).astype(jnp.float32).T
+    grad_proj = later_rows_flow.result[1].reshape(width, model_width).astype(jnp.float32)
     grad_qkv = jnp.transpose(
-        sum_rows(
-            by_share(
-                lax.dot_general(
-                    d_qkv, attn_in, (((0,), (0,)), ((), ())), preferred_element_type=jnp.float32
-                )
+        qkv_rows_flow.result[0].reshape(SHARES, 3, slot, model_width).astype(jnp.float32), (3, 1, 0, 2)
+    ).reshape(model_width, 3, width)
+
+    d_modulation = jnp.stack(
+        [
+            jnp.stack(grad_shift1, 0),
+            jnp.stack(grad_scale1, 0),
+            grad_gate1,
+            grad_shift2,
+            grad_scale2,
+            grad_gate2,
+        ],
+        1,
+    ).astype(jnp.bfloat16)
+    qkv_true = xor_order(
+        qkv_bias_part.reshape(GROUPS, 3, 2, 2, 2, slot), place, (2, 3, 4)
+    ).reshape(GROUPS, 3 * width)
+    d_mod_parts = d_modulation.reshape(latents, 6, GROUPS, width)
+    got = group_send(
+        [
+            jnp.concatenate(
+                [
+                    lax.dynamic_index_in_dim(d_mod_parts, me ^ mask, 2, keepdims=False).reshape(
+                        latents * 6 * width
+                    ),
+                    qkv_true[mask].astype(jnp.bfloat16),
+                ]
             )
-        ).reshape(3, width, model_width),
-        (2, 0, 1),
-    )
-    d_attn_in = jnp.dot(d_qkv, qkv_rows, preferred_element_type=jnp.float32).reshape(
-        latents, seq, model_width
-    )
-    grad_shift1 = jnp.sum(d_attn_in, 1)
-    grad_scale1 = jnp.sum(d_attn_in * norm1, 1)
-    grad_tokens = to_tokens(
-        (d_mid + norm_back(d_attn_in * (1.0 + scale1), norm1, inverse1)).astype(jnp.bfloat16)
-    ).astype(jnp.float32)
-
-    d_modulation = jnp.stack(
-        [grad_shift1, grad_scale1, grad_gate1, grad_shift2, grad_scale2, grad_gate2], 1
-    ).astype(jnp.bfloat16)
-    d_mod_group = lax.all_to_all(d_modulation, "tensor", 2, 0, tiled=True).reshape(
+            for mask in range(GROUPS)
+        ]
+    )
+    d_mod_group = jnp.stack([piece[: latents * 6 * width] for piece in got], 0).reshape(
         group_latents, 6 * width
     )
-    d_mod_all = lax.all_gather(d_mod_group, "dp", axis=0, tiled=True)
-    cond_all = lax.all_gather(cond, "dp", axis=0, tiled=True)
-    silu_all = jax.nn.silu(cond_all.astype(jnp.float32)).astype(jnp.bfloat16)
+    qkv_group = group_add([piece[latents * 6 * width :] for piece in got]).astype(jnp.bfloat16)
+
+    def member_order(array):
+        return xor_order(
+            array.reshape(2, 2, latents, model_width), me, (0, 1)
+        ).reshape(group_latents, model_width)
+
+    everyone = lax.all_gather(
+        jnp.concatenate(
+            [d_mod_group, member_order(silu_c), qkv_group.reshape(group_latents, -1)], 1
+        ),
+        "dp",
+        axis=0,
+    )
+    d_mod_all = everyone[:, :, : 6 * width].reshape(-1, 6 * width)
+    silu_all = everyone[:, :, 6 * width : 6 * width + model_width].reshape(-1, model_width)
+    grad_qv_bias = jnp.sum(
+        everyone[:, :, 6 * width + model_width :].reshape(-1, 3, width).astype(jnp.float32), 0
+    )[::2]
     grad_ada_bias = jnp.sum(d_mod_all.astype(jnp.float32), 0).reshape(6, width)
-    grad_ada = lax.dot_general(
-        silu_all, d_mod_all, (((0,), (0,)), ((), ())), preferred_element_type=jnp.float32
-    ).reshape(model_width, 6, width)
-    d_silu = lax.psum(_nt(d_mod_group, ada_flat).astype(jnp.bfloat16), "tensor").astype(
-        jnp.float32
-    )
+    grad_ada = contract(silu_all, d_mod_all).reshape(model_width, 6, width)
+    d_silu = member_order(_nt(d_mod_group, ada_flat).astype(jnp.bfloat16))
+    d_silu = group_add(group_send([d_silu] * GROUPS))
     grad_cond = jax.vjp(jax.nn.silu, cond_float)[1](d_silu)[0]
-
-    biases = lax.psum(
-        jnp.concatenate([fc2_bias_part, proj_bias_part, fc1_bias_part, qkv_bias_part]).astype(
-            jnp.bfloat16
-        ),
-        ("dp", "tensor"),
-    ).astype(jnp.float32)
-    grad_fc2_bias = biases[:model_width]
-    grad_proj_bias = biases[model_width : 2 * model_width]
-    at = 2 * model_width
-    grad_fc1_bias = lax.dynamic_slice_in_dim(
-        biases[at : at + hidden * groups].reshape(-1, groups, hidden // lax.axis_size("dp")),
-        me,
-        1,
-        1,
-    ).reshape(hidden)
-    at = at + hidden * groups
-    grad_qv_bias = lax.dynamic_slice_in_dim(biases, at + me * 3 * width, 3 * width, 0).reshape(
-        3, width
-    )[::2]
+    grad_fc1_bias = biases.result[:hidden]
+    grad_fc2_bias = biases.result[hidden : hidden + model_width]
+    grad_proj_bias = biases.result[hidden + model_width :]
     return (
         output,
         grad_tokens,
@@ -682,7 +975,12 @@
 
 
 def shards(tokens, cond, cotangent, qkv_weight, *rest):
-    even = tokens.shape[1] % lax.axis_size("tensor") == 0 and qkv_weight.shape[2] % LANES == 0
+    even = (
+        lax.axis_size("tensor") == GROUPS
+        and lax.axis_size("dp") == SHARES
+        and tokens.shape[1] % GROUPS == 0
+        and qkv_weight.shape[2] == 4 * HD
+    )
     program = whole_latents if even else split_heads
     return program(tokens, cond, cotangent, qkv_weight, *rest)
 

time: 1310 us -> 1020 us (0.78)
  waiting for transfers between devices: 373 us -> 133 us
  blocking collectives: 249 us -> 9.15 us
  starting transfers between devices: 24.9 us -> 111 us
  other arithmetic: 90.6 us -> 168 us
  local copies, waits for them, and re-layouts: 103 us -> 152 us
  matrix products: 279 us -> 245 us
    reduce_scatter x8 -> x0, waiting for transfers between devices: 258 us -> none  [the longest x4 158 us: sum_rows(): lax.psum_scatter(whole.astype(jnp.bfloat16), 'dp', scatter_dimension=0, t...]
    all_gather x6 -> x1, blocking collectives: 153 us -> 9.15 us  [whole_latents(): lax.all_gather(jnp.concatenate([d_mod_group, member_order(silu_c), qkv_gr...]
    ppermute x0 -> x79, waiting for transfers between devices: none -> 103 us  [xor_permute(): lax.ppermute(array, axis, [(index, index ^ mask) for index in range(size)])]
    psum x2 -> x0, blocking collectives: 96.3 us -> none  [the longest x1 78.6 us: whole_latents(): lax.psum(jnp.concatenate([fc2_bias_part, proj_bias_part, fc1_bias_part, q...]
    all_to_all x4 -> x7, waiting for transfers between devices: 115 us -> 30.6 us  [exchange(): return lax.all_to_all(pieces, 'tensor', 0, 0)]
    ppermute x0 -> x79, starting transfers between devices: none -> 79.8 us  [xor_permute(): lax.ppermute(array, axis, [(index, index ^ mask) for index in range(size)])]
    convert_element_type x6 -> x45, other arithmetic: 13 us -> 92.7 us  [the longest x1 33.6 us: whole_latents(): jax.vjp(partial(jax.nn.gelu, approximate=True), pre)[1](d_act)[0]]
    reshape x1 -> x22, local copies, waits for them, and re-layouts: 0.01 us -> 32.9 us  [the longest x4 23.4 us: split_tokens(): array.reshape(row_count, GROUPS, latents, model_width)]
  transfers between devices with their start and end apart: 20 -> 89, of which waited for: 7 -> 29; matrix products, arithmetic and copies ran while one was open for 21% -> 38% of each run, Pallas kernels for 5% -> 18%
where the time goes in v2:
time: 1020 us; the launch traced here: 1010 us
  matrix products  245 us (24%)
  Pallas kernels  178 us (17%)
  other arithmetic  168 us (16%)
  local copies, waits for them, and re-layouts  152 us (15%)
  waiting for transfers between devices  133 us (13%)
  starting transfers between devices  111 us (11%)
  between operations  17.2 us (2%)
    ppermute x79, waiting for transfers between devices, xor_permute(): lax.ppermute(array, axis, [(index, index ^ mask) for index in range(size)])  103 us
    pallas_call x2, Pallas kernels, attend_back(): pl.pallas_call(partial(_attend_back_kernel, width=width, rows=min(256, se...  101 us
    dot_general x6, matrix products, _nt(): lax.dot_general(left, right, (((1,), (1,)), ((), ())), preferred_element_...  87.6 us
    ppermute x79, starting transfers between devices, xor_permute(): lax.ppermute(array, axis, [(index, index ^ mask) for index in range(size)])  79.8 us
    dot_general x6, matrix products, contract(): lax.dot_general(left, right, (((0,), (0,)), ((), ())), preferred_element_...  77.1 us
    pallas_call x2, Pallas kernels, attend(): pl.pallas_call(partial(_attend_kernel, width=width, rows=min(256, seq)),...  69.8 us
    unnamed x295, local copies, waits for them, and re-layouts  46.9 us
    convert_element_type x1, other arithmetic, whole_latents(): jax.vjp(partial(jax.nn.gelu, approximate=True), pre)[1](d_act)[0]  33.6 us
  transfers between devices with their start and end apart: 89, of which 29 were waited for; matrix products, arithmetic and copies ran while one was open for 38% of the time, Pallas kernels for 18%

profile of v2, /device:TPU:0, one launch (start us, length us, event | category | flops | bytes accessed | tf_op | source)
XLA Modules:
  0.0 1013.8 jit_solution(374133590692537140)
XLA Ops:
  119.6 24.1 %all-to-all-done = bf16[4,256,1024]{2,1,0:T(8,128)(2,1)S(1)} async-done(((bf16[4,256,1024]{2,1,0:T(8,128)(2,1)}), bf16[4,256,1024]{2,1,0:T(8,128)(2,1)S(1)}, u32[]{:S(2)}, u32[]{:S(2)}) %all-to-all-start) | async-done | bytes 2097184 | tf_op jit(solution)/shard_map/all_to_all | solution.py:645
  153.7 11.5 %add_convert_fusion.2.qkv_ref = bf16[1024,3072]{1,0:T(8,128)(2,1)} fusion(f32[3072]{0:T(1024)S(1)} %add.398, bf16[1024,1024]{1,0:T(8,128)(2,1)S(1)} %add_convert_fusion.9, bf16[3072,1024]{1,0:T(8,128)(2,1)} %bitcast.487), kind=kOutput, calls=%fused_computation.27 | convolution fusion | flops 6448742400 | bytes 14692352 | tf_op jit(solution)/shard_map/dot_general | solution.py:308
  176.8 34.9 %attend.2 = (bf16[1024,1024]{1,0:T(8,128)(2,1)S(1)}, f32[1024,512]{1,0:T(8,128)S(1)}) custom-call(bf16[1024,3072]{1,0:T(8,128)(2,1)S(1)} %copy-done.3), custom_call_target="tpu_custom_call" | custom-call | flops 17179869184 | bytes 10485760 | tf_op jit(solution)/shard_map/attend/pallas_call | solution.py:350
  233.1 8.7 add_convert_fusion.1.qkv_ref
  255.5 34.9 %attend.3 = (bf16[1024,1024]{1,0:T(8,128)(2,1)S(1)}, f32[1024,512]{1,0:T(8,128)S(1)}) custom-call(bf16[1024,3072]{1,0:T(8,128)(2,1)S(1)} %copy-done.2), custom_call_target="tpu_custom_call" | custom-call | flops 17179869184 | bytes 10485760 | tf_op jit(solution)/shard_map/attend/pallas_call | solution.py:350
  333.6 35.5 %fusion.14 = (bf16[2048,4096]{1,0:T(8,128)(2,1)}, f32[2048,4096]{1,0:T(8,128)}) fusion(f32[4096]{0:T(1024)S(1)} %bitcast.578, bf16[2048,1024]{1,0:T(8,128)(2,1)} %bitcast.492, bf16[4096,1024]{1,0:T(8,128)(2,1)} %copy-done.99), kind=kOutput, calls=%fused_computation.17 | convolution fusion | flops 17263755264 | bytes 62930944 | tf_op jit(solution)/shard_map/dot_general | solution.py:308
  377.9 25.7 %convolution_add_fusion.1 = f32[2048,1024]{1,0:T(8,128)} fusion(bf16[2048,4096]{1,0:T(8,128)(2,1)} %get-tuple-element.231, bf16[4096,1024]{1,0:T(8,128)(2,1)S(1)} %constant_dynamic-update-slice_fusion.17, f32[1024]{0:T(1024)S(1)} %copy-done.123), kind=kOutput, calls=%fused_computation.57 | convolution fusion | flops 17181966336 | bytes 33558528 | tf_op jit(solution)/shard_map/dot_general | solution.py:776
  410.2 24.6 %convolution_convert_fusion.1 = bf16[4096,1024]{1,0:T(8,128)(2,1)} fusion(bf16[2048,4096]{1,0:T(8,128)(2,1)} %get-tuple-element.231, bf16[2048,1024]{1,0:T(8,128)(2,1)S(1)} %bitcast.471), kind=kOutput, calls=%fused_computation.44 | convolution fusion | flops 17184063488 | bytes 29360128 | tf_op jit(solution)/shard_map/dot_general | solution.py:648
  452.9 23.1 %fusion.74 = f32[2048,4096]{1,0:T(8,128)} fusion(bf16[2048,1024]{1,0:T(8,128)(2,1)S(1)} %bitcast.473, bf16[4096,1024]{1,0:T(8,128)(2,1)} %copy-done.100), kind=kOutput, calls=%fused_computation.402 | convolution fusion | flops 17179869184 | bytes 46137344 | tf_op jit(solution)/shard_map/dot_general | solution.py:308
  476.0 33.6 %fusion.6 = bf16[2048,4096]{1,0:T(8,128)(2,1)} fusion(f32[2048,4096]{1,0:T(8,128)} %get-tuple-element.244, f32[2048,4096]{1,0:T(8,128)} %fusion.74), kind=kLoop, calls=%fused_computation.9 | loop fusion | flops 167772160 | bytes 83886080 | tf_op jit(solution)/shard_map/convert_element_type | solution.py:792
  524.9 20.4 %convolution_convert_fusion = bf16[4096,1024]{1,0:T(8,128)(2,1)} fusion(bf16[2048,4096]{1,0:T(8,128)(2,1)S(1)} %copy-done.13, bf16[2048,1024]{1,0:T(8,128)(2,1)S(1)} %bitcast.493), kind=kOutput, calls=%fused_computation.43 | convolution fusion | flops 17184063488 | bytes 29360128 | tf_op jit(solution)/shard_map/dot_general | solution.py:648
  560.6 23.1 %fusion.75 = f32[2048,1024]{1,0:T(8,128)S(1)} fusion(bf16[2048,4096]{1,0:T(8,128)(2,1)} %fusion.6, bf16[4096,1024]{1,0:T(8,128)(2,1)} %copy-done.99), kind=kOutput, calls=%fused_computation.403 | convolution fusion | flops 17179869184 | bytes 33554432 | tf_op jit(solution)/shard_map/dot_general | solution.py:798
  607.7 8.1 convolution_convert_fusion.3
  662.4 50.2 %attend_back.2 = bf16[1024,3072]{1,0:T(8,128)(2,1)} custom-call(bf16[1024,3072]{1,0:T(8,128)(2,1)} %add_convert_fusion.2.qkv_ref, bf16[1024,1024]{1,0:T(8,128)(2,1)S(1)} %copy-done.1, f32[1024,512]{1,0:T(8,128)S(1)} %copy-done.7, bf16[1024,1024]{1,0:T(8,128)(2,1)} %get-tuple-element.382.grad_ref), custom_call_target="tpu_custom_call" | custom-call | flops 42949672960 | bytes 18874368 | tf_op jit(solution)/shard_map/attend_back/pallas_call | solution.py:445
  717.3 12.5 %multiply_reduce_fusion.6 = (bf16[1024]{0:T(1024)(128)(2,1)S(1)}, f32[1024]{0:T(1024)S(1)}, f32[1024]{0:T(1024)S(1)}, bf16[1024]{0:T(1024)(128)(2,1)S(1)}, f32[1024,1024]{1,0:T(8,128)S(1)}) fusion(bf16[4,256,1024]{2,1,0:T(8,128)(2,1)} %copy-done.10, f32[1024]{0:T(1024)S(1)} %bitcast.568, f32[1024]{0:T(1024)S(1)} %bitcast.565, f32[1024]{0:T(1024)S(1)} %bitcast.574, ...), kind=kOutput, calls=%fused_computation.75 | convolution fusion | flops 6452932608 | bytes 18898944 | tf_op jit(solution)/shard_map/dot_general | solution.py:872
  729.9 9.4 fusion.76
  750.3 11.5 %collective-permute-done.61 = bf16[2,32,1024]{2,1,0:T(8,128)(2,1)S(1)} collective-permute-done((bf16[2,32,1024]{2,1,0:T(8,128)(2,1)S(1)}, bf16[2,32,1024]{2,1,0:T(8,128)(2,1)S(1)}, u32[]{:S(2)}, u32[]{:S(2)}) %collective-permute-start.61) | collective-permute-done | bytes 131104 | tf_op jit(solution)/shard_map/ppermute | solution.py:471
  792.2 50.5 %attend_back.3 = bf16[1024,3072]{1,0:T(8,128)(2,1)} custom-call(bf16[1024,3072]{1,0:T(8,128)(2,1)} %add_convert_fusion.1.qkv_ref, bf16[1024,1024]{1,0:T(8,128)(2,1)S(1)} %get-tuple-element.209.out_ref, f32[1024,512]{1,0:T(8,128)S(1)} %copy-done.5, bf16[1024,1024]{1,0:T(8,128)(2,1)} %get-tuple-element.287.grad_ref), custom_call_target="tpu_custom_call" | custom-call | flops 42949672960 | bytes 18874368 | tf_op jit(solution)/shard_map/attend_back/pallas_call | solution.py:445
  847.3 11.0 %fusion.77 = f32[3072,1024]{1,0:T(8,128)} fusion(bf16[1024,3072]{1,0:T(8,128)(2,1)S(1)} %copy-done.25, bf16[1024,1024]{1,0:T(8,128)(2,1)} %copy-done.37), kind=kOutput, calls=%fused_computation.405 | convolution fusion | flops 6442450944 | bytes 20971520 | tf_op jit(solution)/shard_map/dot_general | solution.py:648
  858.5 9.2 add_convert_fusion
  869.1 13.1 %multiply_reduce_fusion.5 = (bf16[1024]{0:T(1024)(128)(2,1)S(1)}, f32[1024]{0:T(1024)S(1)}, f32[1024]{0:T(1024)S(1)}, bf16[1024]{0:T(1024)(128)(2,1)S(1)}, f32[1024,1024]{1,0:T(8,128)}) fusion(bf16[4,256,1024]{2,1,0:T(8,128)(2,1)} %all-to-all-done.1, f32[1024]{0:T(1024)S(1)} %bitcast.562, f32[1024]{0:T(1024)S(1)} %bitcast.559, f32[1024]{0:T(1024)S(1)} %bitcast.571, ...), kind=kOutput, calls=%fused_computation.74 | convolution fusion | flops 6452932608 | bytes 18898944 | tf_op jit(solution)/shard_map/dot_general | solution.py:872
  913.5 8.5 collective-permute-done.67
  944.2 11.0 %collective-permute-done.71 = bf16[2,96,1024]{2,1,0:T(8,128)(2,1)} collective-permute-done((bf16[2,96,1024]{2,1,0:T(8,128)(2,1)S(1)}, bf16[2,96,1024]{2,1,0:T(8,128)(2,1)}, u32[]{:S(2)}, u32[]{:S(2)}) %collective-permute-start.71) | collective-permute-done | bytes 393248 | tf_op jit(solution)/shard_map/ppermute | solution.py:471
  977.4 9.2 all-gather.3
  (746 shorter events, 492.5 us)
Async XLA Ops:
  8.6 66.8 %collective-permute-start.16 = (bf16[1536]{0:T(1024)(128)(2,1)S(1)}, bf16[1536]{0:T(1024)(128)(2,1)S(1)}, u32[]{:S(2)}, u32[]{:S(2)}) collective-permute-start(bf16[1536]{0:T(1024)(128)(2,1)S(1)} %constant_dynamic-update-slice_fusion.31), channel_id=1, source_target_pairs={{0,3},{1,2},{2,1},{3,0},{4,7},{5,6},{6,5},{7,4},{8,11},{9,10},{10,... | collective-permute-start | bytes 9224 | tf_op jit(solution)/shard_map/ppermute | solution.py:471
  13.6 62.1 %collective-permute-start.15 = (bf16[1536]{0:T(1024)(128)(2,1)S(1)}, bf16[1536]{0:T(1024)(128)(2,1)S(1)}, u32[]{:S(2)}, u32[]{:S(2)}) collective-permute-start(bf16[1536]{0:T(1024)(128)(2,1)S(1)} %constant_dynamic-update-slice_fusion.31), channel_id=1, source_target_pairs={{0,2},{1,3},{2,0},{3,1},{4,6},{5,7},{6,4},{7,5},{8,10},{9,11},{10,... | collective-permute-start | bytes 9224 | tf_op jit(solution)/shard_map/ppermute | solution.py:471
  13.6 63.6 %collective-permute-start.14 = (bf16[1536]{0:T(1024)(128)(2,1)S(1)}, bf16[1536]{0:T(1024)(128)(2,1)S(1)}, u32[]{:S(2)}, u32[]{:S(2)}) collective-permute-start(bf16[1536]{0:T(1024)(128)(2,1)S(1)} %constant_dynamic-update-slice_fusion.31), channel_id=1, source_target_pairs={{0,1},{1,0},{2,3},{3,2},{4,5},{5,4},{6,7},{7,6},{8,9},{9,8},{10,11... | collective-permute-start | bytes 9224 | tf_op jit(solution)/shard_map/ppermute | solution.py:471
  16.9 45.9 %collective-permute-start.4 = (bf16[128,1024]{1,0:T(8,128)(2,1)S(1)}, bf16[128,1024]{1,0:T(8,128)(2,1)S(1)}, u32[]{:S(2)}, u32[]{:S(2)}) collective-permute-start(bf16[128,1024]{1,0:T(8,128)(2,1)S(1)} %pad_maximum_fusion.26), channel_id=1, source_target_pairs={{0,2},{1,3},{2,0},{3,1},{4,6},{5,7},{6,4},{7,5},{8,10},{9,11},{10,... | collective-permute-start | bytes 786440 | tf_op jit(solution)/shard_map/ppermute | solution.py:471
  19.3 45.8 %collective-permute-start.3 = (bf16[128,1024]{1,0:T(8,128)(2,1)S(1)}, bf16[128,1024]{1,0:T(8,128)(2,1)S(1)}, u32[]{:S(2)}, u32[]{:S(2)}) collective-permute-start(bf16[128,1024]{1,0:T(8,128)(2,1)S(1)} %pad_maximum_fusion.26), channel_id=1, source_target_pairs={{0,1},{1,0},{2,3},{3,2},{4,5},{5,4},{6,7},{7,6},{8,9},{9,8},{10,11... | collective-permute-start | bytes 786440 | tf_op jit(solution)/shard_map/ppermute | solution.py:471
  92.4 51.3 %all-to-all-start = ((bf16[4,256,1024]{2,1,0:T(8,128)(2,1)}), bf16[4,256,1024]{2,1,0:T(8,128)(2,1)S(1)}, u32[]{:S(2)}, u32[]{:S(2)}) async-start(bf16[4,256,1024]{2,1,0:T(8,128)(2,1)} %get-tuple-element.174), calls=%async_computation | async-start | bytes 4194304 | tf_op jit(solution)/shard_map/all_to_all | solution.py:645
  165.3 53.3 %all-to-all-start.1 = ((bf16[4,256,1024]{2,1,0:T(8,128)(2,1)}), bf16[4,256,1024]{2,1,0:T(8,128)(2,1)}, u32[]{:S(2)}, u32[]{:S(2)}) async-start(bf16[4,256,1024]{2,1,0:T(8,128)(2,1)} %get-tuple-element.187), calls=%async_computation.1 | async-start | bytes 4194304 | tf_op jit(solution)/shard_map/all_to_all | solution.py:645
  244.1 52.8 %all-to-all-start.2 = ((bf16[4,256,1024]{2,1,0:T(8,128)(2,1)}), bf16[4,256,1024]{2,1,0:T(8,128)(2,1)}, u32[]{:S(2)}, u32[]{:S(2)}) async-start(bf16[4,256,1024]{2,1,0:T(8,128)(2,1)} %get-tuple-element.198), calls=%async_computation.2 | async-start | bytes 4194304 | tf_op jit(solution)/shard_map/all_to_all | solution.py:645
  300.9 68.2 %all-to-all-start.3 = ((bf16[4,256,1024]{2,1,0:T(8,128)(2,1)}), bf16[4,256,1024]{2,1,0:T(8,128)(2,1)}, u32[]{:S(2)}, u32[]{:S(2)}) async-start(bf16[4,256,1024]{2,1,0:T(8,128)(2,1)} %get-tuple-element.230), calls=%async_computation.3 | async-start | bytes 4194304 | tf_op jit(solution)/shard_map/all_to_all | solution.py:645
  322.1 47.0 %collective-permute-start.38 = (bf16[3,128,1024]{2,1,0:T(8,128)(2,1)}, bf16[3,128,1024]{2,1,0:T(8,128)(2,1)}, u32[]{:S(2)}, u32[]{:S(2)}) collective-permute-start(bf16[3,128,1024]{2,1,0:T(8,128)(2,1)} %constant_dynamic-update-slice_fusion.15), channel_id=1, source_target_pairs={{0,4},{4,0},{8,12},{12,8},{16,20},{20,16},{24,28},{28,24},{1,5},{5... | collective-permute-start | bytes 2359304 | tf_op jit(solution)/shard_map/ppermute | solution.py:471
  441.3 108.1 %all-to-all-start.4 = ((bf16[4,2,256,1024]{3,2,1,0:T(8,128)(2,1)}), bf16[4,2,256,1024]{3,2,1,0:T(8,128)(2,1)}, u32[]{:S(2)}, u32[]{:S(2)}) async-start(bf16[4,2,256,1024]{3,2,1,0:T(8,128)(2,1)} %bitcast.467), calls=%async_computation.4 | async-start | bytes 8388608 | tf_op jit(solution)/shard_map/all_to_all | solution.py:645
  446.4 270.9 %all-gather.8.cloned.1.call-start = ((), (), s32[]{:S(2)}) async-start(), calls=%async_computation.7 | async-start | bytes 2359296 | tf_op jit(solution)/shard_map/all_gather | solution.py:597
  452.9 56.7 %collective-permute-start.39 = (bf16[4,4,128,1024]{3,2,1,0:T(8,128)(2,1)}, bf16[4,4,128,1024]{3,2,1,0:T(8,128)(2,1)}, u32[]{:S(2)}, u32[]{:S(2)}) collective-permute-start(bf16[4,4,128,1024]{3,2,1,0:T(8,128)(2,1)} %bitcast.90), channel_id=1, source_target_pairs={{0,4},{4,0},{8,12},{12,8},{16,20},{20,16},{24,28},{28,24},{1,5},{5... | collective-permute-start | bytes 12582920 | tf_op jit(solution)/shard_map/ppermute | solution.py:471
  634.4 78.2 %collective-permute-start.54 = (bf16[3072]{0:T(1024)(128)(2,1)S(1)}, bf16[3072]{0:T(1024)(128)(2,1)S(1)}, u32[]{:S(2)}, u32[]{:S(2)}) collective-permute-start(bf16[3072]{0:T(1024)(128)(2,1)S(1)} %get-tuple-element.467), channel_id=1, source_target_pairs={{0,1},{1,0},{2,3},{3,2},{4,5},{5,4},{6,7},{7,6},{8,9},{9,8},{10,11... | collective-permute-start | bytes 18440 | tf_op jit(solution)/shard_map/ppermute | solution.py:471
  649.0 193.7 %all-gather.10.cloned.1.call-start = ((), (), s32[]{:S(2)}) async-start(), calls=%async_computation.8 | async-start | bytes 2949120 | tf_op jit(solution)/shard_map/all_gather | solution.py:597
  653.4 63.8 %collective-permute-start.49 = (bf16[4,64,1024]{2,1,0:T(8,128)(2,1)S(1)}, bf16[4,64,1024]{2,1,0:T(8,128)(2,1)}, u32[]{:S(2)}, u32[]{:S(2)}) collective-permute-start(bf16[4,64,1024]{2,1,0:T(8,128)(2,1)S(1)} %get-tuple-element.427), channel_id=1, source_target_pairs={{0,16},{4,20},{8,24},{12,28},{16,0},{20,4},{24,8},{28,12},{1,17},{... | collective-permute-start | bytes 1572872 | tf_op jit(solution)/shard_map/ppermute | solution.py:471
  656.2 61.0 %collective-permute-start.50 = (bf16[4,64,1024]{2,1,0:T(8,128)(2,1)S(1)}, bf16[4,64,1024]{2,1,0:T(8,128)(2,1)}, u32[]{:S(2)}, u32[]{:S(2)}) collective-permute-start(bf16[4,64,1024]{2,1,0:T(8,128)(2,1)S(1)} %get-tuple-element.425), channel_id=1, source_target_pairs={{0,8},{4,12},{8,0},{12,4},{16,24},{20,28},{24,16},{28,20},{1,9},{5... | collective-permute-start | bytes 1572872 | tf_op jit(solution)/shard_map/ppermute | solution.py:471
  660.2 57.0 %collective-permute-start.53 = (bf16[2,4,16,1024]{3,2,1,0:T(8,128)(2,1)S(1)}, bf16[2,4,16,1024]{3,2,1,0:T(8,128)(2,1)S(1)}, u32[]{:S(2)}, u32[]{:S(2)}) collective-permute-start(bf16[2,4,16,1024]{3,2,1,0:T(8,128)(2,1)S(1)} %get-tuple-element.423), channel_id=1, source_target_pairs={{0,16},{4,20},{8,24},{12,28},{16,0},{20,4},{24,8},{28,12},{1,17},{... | collective-permute-start | bytes 786440 | tf_op jit(solution)/shard_map/ppermute | solution.py:471
  661.3 55.9 %collective-permute-start.52 = (bf16[2,4,16,1024]{3,2,1,0:T(8,128)(2,1)S(1)}, bf16[2,4,16,1024]{3,2,1,0:T(8,128)(2,1)}, u32[]{:S(2)}, u32[]{:S(2)}) collective-permute-start(bf16[2,4,16,1024]{3,2,1,0:T(8,128)(2,1)S(1)} %slice_bitcast_fusion.44), channel_id=1, source_target_pairs={{0,8},{4,12},{8,0},{12,4},{16,24},{20,28},{24,16},{28,20},{1,9},{5... | collective-permute-start | bytes 786440 | tf_op jit(solution)/shard_map/ppermute | solution.py:471
  784.9 57.8 %all-to-all-start.5 = ((bf16[4,256,1024]{2,1,0:T(8,128)(2,1)}), bf16[4,256,1024]{2,1,0:T(8,128)(2,1)}, u32[]{:S(2)}, u32[]{:S(2)}) async-start(bf16[4,256,1024]{2,1,0:T(8,128)(2,1)} %bitcast.484), calls=%async_computation.5 | async-start | bytes 4194304 | tf_op jit(solution)/shard_map/all_to_all | solution.py:645
  789.6 53.1 %collective-permute-start.65 = (bf16[3072]{0:T(1024)(128)(2,1)S(1)}, bf16[3072]{0:T(1024)(128)(2,1)S(1)}, u32[]{:S(2)}, u32[]{:S(2)}) collective-permute-start(bf16[3072]{0:T(1024)(128)(2,1)S(1)} %add_convert_fusion.25), channel_id=1, source_target_pairs={{0,16},{4,20},{8,24},{12,28},{16,0},{20,4},{24,8},{28,12},{1,17},{... | collective-permute-start | bytes 18440 | tf_op jit(solution)/shard_map/ppermute | solution.py:471
  886.8 57.2 %collective-permute-start.74 = (bf16[3840]{0:T(1024)(128)(2,1)S(1)}, bf16[3840]{0:T(1024)(128)(2,1)S(1)}, u32[]{:S(2)}, u32[]{:S(2)}) collective-permute-start(bf16[3840]{0:T(1024)(128)(2,1)S(1)} %pad_maximum_fusion.44), channel_id=1, source_target_pairs={{0,2},{1,3},{2,0},{3,1},{4,6},{5,7},{6,4},{7,5},{8,10},{9,11},{10,... | collective-permute-start | bytes 23048 | tf_op jit(solution)/shard_map/ppermute | solution.py:471
  909.4 60.0 %all-to-all-start.6 = ((bf16[4,256,1024]{2,1,0:T(8,128)(2,1)}), bf16[4,256,1024]{2,1,0:T(8,128)(2,1)S(1)}, u32[]{:S(2)}, u32[]{:S(2)}) async-start(bf16[4,256,1024]{2,1,0:T(8,128)(2,1)} %bitcast.483), calls=%async_computation.6 | async-start | bytes 4194304 | tf_op jit(solution)/shard_map/all_to_all | solution.py:645
  913.5 86.0 %all-gather.12.cloned.1.call-start = ((), (), s32[]{:S(2)}) async-start(), calls=%async_computation.9 | async-start | bytes 1769472 | tf_op jit(solution)/shard_map/all_gather | solution.py:597
  (197 other events, 2706.7 us)
Sparse Core Ops, SparseCore 0:
  649.2 35.4 all-gather.7
  780.9 28.9 all-gather.9
  970.4 24.3 all-gather.11

commit v3 on v2

--- a/solution.py
+++ b/solution.py
@@ -481,6 +481,28 @@
     return (left.astype(jnp.float32) + right.astype(jnp.float32)).astype(jnp.bfloat16)
 
 
+def _split_kernel(array_ref, *piece_refs):
+    by_latent = jnp.swapaxes(array_ref[...].astype(jnp.float32), 0, 1).astype(jnp.bfloat16)
+    latents = len(piece_refs)
+    for index, piece_ref in enumerate(piece_refs):
+        for member in range(GROUPS):
+            piece_ref[member] = by_latent[member * latents + index]
+
+
+def split_latents(array, latents):
+    count, _, depth = array.shape
+    step = 32
+    return pl.pallas_call(
+        _split_kernel,
+        grid=(count // step,),
+        in_specs=[pl.BlockSpec((step, GROUPS * latents, depth), lambda i: (i, 0, 0))],
+        out_specs=[pl.BlockSpec((GROUPS, step, depth), lambda i: (0, i, 0))] * latents,
+        out_shape=[jax.ShapeDtypeStruct((GROUPS, count, depth), jnp.bfloat16)] * latents,
+        cost_estimate=pl.CostEstimate(flops=0, bytes_accessed=4 * array.size, transcendentals=0),
+        name="split_latents",
+    )(array)
+
+
 def _merge_kernel(*refs):
     *piece_refs, array_ref = refs
     pieces = [ref[member] for member in range(GROUPS) for ref in piece_refs]
@@ -528,10 +550,13 @@
     return array
 
 
-def gather_local(mine, shares, pauses):
+def gather_local(mine, shares, pauses, direct=False):
     place = lax.axis_index("dp")
     near, far = xor_permute(mine, "tensor", 1), xor_permute(mine, "tensor", 2)
-    got = (near, far, xor_permute(far, "tensor", 1))
+    if direct:
+        got = (near, far, xor_permute(mine, "tensor", 3))
+    else:
+        got = (near, far, xor_permute(far, "tensor", 1))
     if 0 in pauses:
         got = yield got
     block = jnp.stack(got, 0)
@@ -636,10 +661,7 @@
     me, place = lax.axis_index("tensor"), lax.axis_index("dp")
 
     def split_tokens(array):
-        pieces = jnp.transpose(
-            array.reshape(row_count, GROUPS, latents, model_width), (1, 2, 0, 3)
-        )
-        return [pieces[:, index] for index in range(latents)]
+        return split_latents(array, latents)
 
     def exchange(pieces):
         return lax.all_to_all(pieces, "tensor", 0, 0)
@@ -667,15 +689,7 @@
         ],
         0,
     )
-    weights = Flow(gather_local(own_attention, attention_shares, (0,)))
-    pieces = window(split_tokens(tokens), weights)
-    incoming = [Flow(sent(pieces[0], exchange))]
-    grad_pieces = split_tokens(cotangent)
-    fc1_shares = fc1_weight.T.reshape(SHARES, part, model_width)
-    fc2_shares = fc2_weight.reshape(SHARES, part, model_width)
-    own_fc1 = lax.dynamic_index_in_dim(fc1_shares, place, 0, keepdims=False)
-    own_fc2 = lax.dynamic_index_in_dim(fc2_shares, place, 0, keepdims=False)
-
+    weights = Flow(gather_local(own_attention, attention_shares, (0,), True))
     cond_float = cond.astype(jnp.float32)
     silu_c = jax.nn.silu(cond_float).astype(jnp.bfloat16)
     ada_flat = ada_weight.reshape(model_width, 6 * width)
@@ -687,6 +701,16 @@
     for mask in range(GROUPS):
         piece = lax.dynamic_index_in_dim(mod_part, me ^ mask, 0, keepdims=False)
         mod_got.append(xor_permute(piece, "tensor", mask) if mask else piece)
+    pieces, mod_got, cotangent, fc1_weight, fc2_weight = window(
+        (split_tokens(tokens), mod_got, cotangent, fc1_weight, fc2_weight), weights
+    )
+    incoming = [Flow(sent(pieces[0], exchange))]
+    grad_pieces = split_tokens(cotangent)
+    fc1_shares = fc1_weight.T.reshape(SHARES, part, model_width)
+    fc2_shares = fc2_weight.reshape(SHARES, part, model_width)
+    own_fc1 = lax.dynamic_index_in_dim(fc1_shares, place, 0, keepdims=False)
+    own_fc2 = lax.dynamic_index_in_dim(fc2_shares, place, 0, keepdims=False)
+
     modulation = xor_order(jnp.stack(mod_got, 0).reshape(2, 2, latents, 6, width), me, (0, 1))
     modulation = jnp.transpose(
         modulation.reshape(GROUPS, latents, 6, width), (1, 2, 0, 3)
@@ -706,7 +730,10 @@
         GROUPS * 3 * width
     )
 
-    modulation, attention_shares = window((modulation, attention_shares), weights)
+    (modulation, attention_shares, grad_pieces, fc1_shares, own_fc1) = window(
+        (modulation, attention_shares, grad_pieces, fc1_shares, own_fc1), weights
+    )
+    fc1_flow = Flow(gather_local(own_fc1, fc1_shares, (0, 1, 2)))
     attention_all = jnp.stack([jnp.stack(chips, 0) for chips in weights.result], 0)
     qkv_rows = jnp.transpose(
         attention_all[:, :, :, : 3 * slot].reshape(2, 4, GROUPS, 3, slot, model_width),
@@ -715,15 +742,13 @@
     proj_rows = jnp.transpose(attention_all[:, :, :, 3 * slot :], (2, 1, 0, 3, 4)).reshape(
         GROUPS * width, model_width
     )
-    (modulation, qkv_rows, proj_rows, pieces, grad_pieces, fc1_shares, own_fc1, own_fc2) = window(
-        (modulation, qkv_rows, proj_rows, pieces, grad_pieces, fc1_shares, own_fc1, own_fc2),
-        incoming[0],
+    (modulation, qkv_rows, proj_rows, pieces, grad_pieces, own_fc2) = window(
+        (modulation, qkv_rows, proj_rows, pieces, grad_pieces, own_fc2), incoming[0]
     )
     modulation = modulation.astype(jnp.float32)
     shift1, scale1, gate1, shift2, scale2, gate2 = [
         modulation[:, index][:, None] for index in range(6)
     ]
-    fc1_flow = Flow(gather_local(own_fc1, fc1_shares, (0, 1, 2)))
     tokens_in, attn_in, qkv, attended, log_totals = [], [], [], [], []
     for index in range(latents):
         tokens_in.append(incoming[index].result.reshape(seq, model_width))
@@ -868,15 +893,19 @@
                 (3, 2, 0, 1, 4, 5),
             ).reshape(2, 4, GROUPS, 3 * slot, model_width)
             d_qkv[index], qkv_blocks = lax.optimization_barrier((d_qkv[index], qkv_blocks))
-            qkv_sum = Flow(reduce_local(qkv_blocks, (0,)))
+            qkv_sum = Flow(reduce_local(qkv_blocks, (0, 1, 2)))
         d_attn_in = jnp.dot(d_qkv[index], qkv_rows, preferred_element_type=jnp.float32)
+        if last:
+            d_attn_in = window(d_attn_in, qkv_sum)
         norm1, inverse1 = layer_stats(tokens_in[index].astype(jnp.float32))
         grad_shift1.append(jnp.sum(d_attn_in, 0))
         grad_scale1.append(jnp.sum(d_attn_in * norm1, 0))
         local = d_mid[index] + norm_back(d_attn_in * (1.0 + scale1[index]), norm1, inverse1)
         local = local.astype(jnp.bfloat16).reshape(GROUPS, row_count, model_width)
         if last:
-            local = window(local, qkv_sum)
+            for _ in range(3):
+                local = window(local, qkv_sum)
+            qkv_rows_flow = Flow(gathered(qkv_sum.result))
         else:
             flows = (fc1_sum, proj_sum, biases)
             (local, d_attended[index + 1], qkv_local) = window(
@@ -885,8 +914,7 @@
         returned.append(Flow(sent(local, exchange)))
         if index == 0:
             later_rows_flow = Flow(gathered(fc1_sum.result, proj_sum.result))
-    window((), qkv_sum, returned[-1])
-    qkv_rows_flow = Flow(gathered(qkv_sum.result))
+    returned[-1].advance(returned[-1].values)
     qkv_rows_flow.advance(qkv_rows_flow.values)
     grad_tokens = merge_latents([flow.result for flow in returned], jnp.float32)
     output = jnp.transpose(out_flow.result, (2, 0, 1, 3)).reshape(

time: 1020 us -> 1040 us (1.020)
  local copies, waits for them, and re-layouts: 152 us -> 131 us
  Pallas kernels: 178 us -> 193 us
  other arithmetic: 168 us -> 181 us
  waiting for transfers between devices: 133 us -> 145 us
    ppermute x79, waiting for transfers between devices: 103 us -> 138 us  [xor_permute(): lax.ppermute(array, axis, [(index, index ^ mask) for index in range(size)])]
    all_to_all x7, waiting for transfers between devices: 30.6 us -> 7.02 us  [exchange(): return lax.all_to_all(pieces, 'tensor', 0, 0)]
    reshape x5 -> x0, local copies, waits for them, and re-layouts: 23.4 us -> none  [the longest x4 23.4 us: split_tokens(): array.reshape(row_count, GROUPS, latents, model_width)]
    pallas_call x0 -> x2, Pallas kernels: none -> 14.9 us  [split_latents(): pl.pallas_call(_split_kernel, grid=(count // step,), in_specs=[pl.BlockSp...]
    convert_element_type x29 -> x30, other arithmetic: 32.1 us -> 34.1 us  [add_low(): (left.astype(jnp.float32) + right.astype(jnp.float32)).astype(jnp.bfloat16)]
    unnamed x295 -> x293, local copies, waits for them, and re-layouts: 46.9 us -> 45.7 us
  transfers between devices with their start and end apart: 89 -> 89, of which waited for: 29 -> 24; matrix products, arithmetic and copies ran while one was open for 38% -> 37% of each run, Pallas kernels for 18% -> 18%
where the time goes in v3:
time: 1040 us; the launch traced here: 1030 us
  matrix products  240 us (23%)
  Pallas kernels  193 us (19%)
  other arithmetic  181 us (17%)
  waiting for transfers between devices  145 us (14%)
  local copies, waits for them, and re-layouts  131 us (13%)
  starting transfers between devices  115 us (11%)
  between operations  17 us (2%)
    ppermute x79, waiting for transfers between devices, xor_permute(): lax.ppermute(array, axis, [(index, index ^ mask) for index in range(size)])  138 us
    pallas_call x2, Pallas kernels, attend_back(): pl.pallas_call(partial(_attend_back_kernel, width=width, rows=min(256, se...  101 us
    dot_general x6, matrix products, _nt(): lax.dot_general(left, right, (((1,), (1,)), ((), ())), preferred_element_...  87.1 us
    ppermute x79, starting transfers between devices, xor_permute(): lax.ppermute(array, axis, [(index, index ^ mask) for index in range(size)])  81.4 us
    dot_general x6, matrix products, contract(): lax.dot_general(left, right, (((0,), (0,)), ((), ())), preferred_element_...  75.6 us
    pallas_call x2, Pallas kernels, attend(): pl.pallas_call(partial(_attend_kernel, width=width, rows=min(256, seq)),...  69.7 us
    unnamed x293, local copies, waits for them, and re-layouts  45.7 us
    convert_element_type x30, other arithmetic, add_low(): (left.astype(jnp.float32) + right.astype(jnp.float32)).astype(jnp.bfloat16)  34.1 us
  transfers between devices with their start and end apart: 89, of which 24 were waited for; matrix products, arithmetic and copies ran while one was open for 37% of the time, Pallas kernels for 18%

profile of v3, /device:TPU:0, one launch (start us, length us, event | category | flops | bytes accessed | tf_op | source)
XLA Modules:
  0.0 1030.3 jit_solution(2253829998686995807)
XLA Ops:
  52.0 13.5 %collective-permute-done.7 = bf16[3,128,1024]{2,1,0:T(8,128)(2,1)S(1)} collective-permute-done((bf16[3,128,1024]{2,1,0:T(8,128)(2,1)S(1)}, bf16[3,128,1024]{2,1,0:T(8,128)(2,1)S(1)}, u32[]{:S(2)}, u32[]{:S(2)}) %collective-permute-start.7) | collective-permute-done | bytes 786464 | tf_op jit(solution)/shard_map/ppermute | solution.py:471
  112.5 18.7 %collective-permute-done.18 = bf16[128,1024]{1,0:T(8,128)(2,1)} collective-permute-done((bf16[128,1024]{1,0:T(8,128)(2,1)}, bf16[128,1024]{1,0:T(8,128)(2,1)}, u32[]{:S(2)}, u32[]{:S(2)}) %collective-permute-start.18) | collective-permute-done | bytes 262176 | tf_op jit(solution)/shard_map/ppermute | solution.py:471
  133.3 12.2 %add_convert_fusion.2.qkv_ref = bf16[1024,3072]{1,0:T(8,128)(2,1)} fusion(f32[3072]{0:T(1024)S(1)} %add.398, bf16[1024,1024]{1,0:T(8,128)(2,1)S(1)} %add_convert_fusion.9, bf16[3072,1024]{1,0:T(8,128)(2,1)} %bitcast.464), kind=kOutput, calls=%fused_computation.27 | convolution fusion | flops 6448742400 | bytes 14692352 | tf_op jit(solution)/shard_map/dot_general | solution.py:308
  156.1 34.9 %attend.2 = (bf16[1024,1024]{1,0:T(8,128)(2,1)S(1)}, f32[1024,512]{1,0:T(8,128)S(1)}) custom-call(bf16[1024,3072]{1,0:T(8,128)(2,1)S(1)} %copy-done.3), custom_call_target="tpu_custom_call" | custom-call | flops 17179869184 | bytes 10485760 | tf_op jit(solution)/shard_map/attend/pallas_call | solution.py:350
  235.0 34.9 %attend.3 = (bf16[1024,1024]{1,0:T(8,128)(2,1)S(1)}, f32[1024,512]{1,0:T(8,128)S(1)}) custom-call(bf16[1024,3072]{1,0:T(8,128)(2,1)S(1)} %copy-done.2), custom_call_target="tpu_custom_call" | custom-call | flops 17179869184 | bytes 10485760 | tf_op jit(solution)/shard_map/attend/pallas_call | solution.py:350
  314.9 35.4 %fusion.14 = (bf16[2048,4096]{1,0:T(8,128)(2,1)}, f32[2048,4096]{1,0:T(8,128)}) fusion(f32[4096]{0:T(1024)S(1)} %bitcast.550, bf16[2048,1024]{1,0:T(8,128)(2,1)} %bitcast.469, bf16[4096,1024]{1,0:T(8,128)(2,1)} %copy-done.96), kind=kOutput, calls=%fused_computation.17 | convolution fusion | flops 17263755264 | bytes 62930944 | tf_op jit(solution)/shard_map/dot_general | solution.py:308
  359.1 25.5 %convolution_add_fusion.1 = f32[2048,1024]{1,0:T(8,128)} fusion(bf16[2048,4096]{1,0:T(8,128)(2,1)} %get-tuple-element.267, bf16[4096,1024]{1,0:T(8,128)(2,1)S(1)} %constant_dynamic-update-slice_fusion.17, f32[1024]{0:T(1024)S(1)} %copy-done.122), kind=kOutput, calls=%fused_computation.57 | convolution fusion | flops 17181966336 | bytes 33558528 | tf_op jit(solution)/shard_map/dot_general | solution.py:801
  391.0 24.6 %convolution_convert_fusion.1 = bf16[4096,1024]{1,0:T(8,128)(2,1)} fusion(bf16[2048,4096]{1,0:T(8,128)(2,1)} %get-tuple-element.267, bf16[2048,1024]{1,0:T(8,128)(2,1)S(1)} %bitcast.449), kind=kOutput, calls=%fused_computation.44 | convolution fusion | flops 17184063488 | bytes 29360128 | tf_op jit(solution)/shard_map/dot_general | solution.py:670
  433.8 23.1 %fusion.67 = f32[2048,4096]{1,0:T(8,128)} fusion(bf16[2048,1024]{1,0:T(8,128)(2,1)S(1)} %bitcast.451, bf16[4096,1024]{1,0:T(8,128)(2,1)} %copy-done.97), kind=kOutput, calls=%fused_computation.392 | convolution fusion | flops 17179869184 | bytes 46137344 | tf_op jit(solution)/shard_map/dot_general | solution.py:308
  456.9 33.6 %fusion.6 = bf16[2048,4096]{1,0:T(8,128)(2,1)} fusion(f32[2048,4096]{1,0:T(8,128)} %get-tuple-element.280, f32[2048,4096]{1,0:T(8,128)} %fusion.67), kind=kLoop, calls=%fused_computation.9 | loop fusion | flops 167772160 | bytes 83886080 | tf_op jit(solution)/shard_map/convert_element_type | solution.py:817
  505.9 20.3 %convolution_convert_fusion = bf16[4096,1024]{1,0:T(8,128)(2,1)} fusion(bf16[2048,4096]{1,0:T(8,128)(2,1)S(1)} %copy-done.13, bf16[2048,1024]{1,0:T(8,128)(2,1)S(1)} %bitcast.470), kind=kOutput, calls=%fused_computation.43 | convolution fusion | flops 17184063488 | bytes 29360128 | tf_op jit(solution)/shard_map/dot_general | solution.py:670
  541.7 22.9 %fusion.68 = f32[2048,1024]{1,0:T(8,128)S(1)} fusion(bf16[2048,4096]{1,0:T(8,128)(2,1)} %fusion.6, bf16[4096,1024]{1,0:T(8,128)(2,1)} %copy-done.96), kind=kOutput, calls=%fused_computation.393 | convolution fusion | flops 17179869184 | bytes 33554432 | tf_op jit(solution)/shard_map/dot_general | solution.py:823
  644.2 50.3 %attend_back.2 = bf16[1024,3072]{1,0:T(8,128)(2,1)} custom-call(bf16[1024,3072]{1,0:T(8,128)(2,1)} %add_convert_fusion.2.qkv_ref, bf16[1024,1024]{1,0:T(8,128)(2,1)S(1)} %copy-done.1, f32[1024,512]{1,0:T(8,128)S(1)} %copy-done.7, bf16[1024,1024]{1,0:T(8,128)(2,1)} %get-tuple-element.428.grad_ref), custom_call_target="tpu_custom_call" | custom-call | flops 42949672960 | bytes 18874368 | tf_op jit(solution)/shard_map/attend_back/pallas_call | solution.py:445
  699.1 12.5 %multiply_reduce_fusion.6 = (bf16[1024]{0:T(1024)(128)(2,1)S(1)}, f32[1024]{0:T(1024)S(1)}, f32[1024]{0:T(1024)S(1)}, bf16[1024]{0:T(1024)(128)(2,1)S(1)}, f32[1024,1024]{1,0:T(8,128)S(1)}) fusion(bf16[4,256,1024]{2,1,0:T(8,128)(2,1)} %copy-done.10, f32[1024]{0:T(1024)S(1)} %bitcast.543, f32[1024]{0:T(1024)S(1)} %bitcast.540, f32[1024]{0:T(1024)S(1)} %bitcast.546, ...), kind=kOutput, calls=%fused_computation.73 | convolution fusion | flops 6452932608 | bytes 18898944 | tf_op jit(solution)/shard_map/dot_general | solution.py:897
  711.7 9.4 fusion.69
  732.5 11.1 %collective-permute-done.61 = bf16[2,32,1024]{2,1,0:T(8,128)(2,1)S(1)} collective-permute-done((bf16[2,32,1024]{2,1,0:T(8,128)(2,1)S(1)}, bf16[2,32,1024]{2,1,0:T(8,128)(2,1)S(1)}, u32[]{:S(2)}, u32[]{:S(2)}) %collective-permute-start.61) | collective-permute-done | bytes 131104 | tf_op jit(solution)/shard_map/ppermute | solution.py:471
  774.0 50.4 %attend_back.3 = bf16[1024,3072]{1,0:T(8,128)(2,1)} custom-call(bf16[1024,3072]{1,0:T(8,128)(2,1)} %add_convert_fusion.1.qkv_ref, bf16[1024,1024]{1,0:T(8,128)(2,1)S(1)} %get-tuple-element.245.out_ref, f32[1024,512]{1,0:T(8,128)S(1)} %copy-done.5, bf16[1024,1024]{1,0:T(8,128)(2,1)} %get-tuple-element.323.grad_ref), custom_call_target="tpu_custom_call" | custom-call | flops 42949672960 | bytes 18874368 | tf_op jit(solution)/shard_map/attend_back/pallas_call | solution.py:445
  834.2 9.4 fusion.70
  843.9 9.2 add_convert_fusion
  864.0 10.6 %fusion.71 = f32[1024,1024]{1,0:T(8,128)S(1)} fusion(bf16[1024,3072]{1,0:T(8,128)(2,1)} %attend_back.3, bf16[3072,1024]{1,0:T(8,128)(2,1)} %bitcast.466), kind=kOutput, calls=%fused_computation.396 | convolution fusion | flops 6442450944 | bytes 16777216 | tf_op jit(solution)/shard_map/dot_general | solution.py:897
  892.0 11.8 %collective-permute-done.67 = bf16[2,4,48,1024]{3,2,1,0:T(8,128)(2,1)S(1)} collective-permute-done((bf16[2,4,48,1024]{3,2,1,0:T(8,128)(2,1)S(1)}, bf16[2,4,48,1024]{3,2,1,0:T(8,128)(2,1)S(1)}, u32[]{:S(2)}, u32[]{:S(2)}) %collective-permute-start.67) | collective-permute-done | bytes 786464 | tf_op jit(solution)/shard_map/ppermute | solution.py:471
  954.6 30.9 %collective-permute-done.78 = bf16[8,1024]{1,0:T(8,128)(2,1)S(1)} collective-permute-done((bf16[8,1024]{1,0:T(8,128)(2,1)S(1)}, bf16[8,1024]{1,0:T(8,128)(2,1)S(1)}, u32[]{:S(2)}, u32[]{:S(2)}) %collective-permute-start.78) | collective-permute-done | bytes 16416 | tf_op jit(solution)/shard_map/ppermute | solution.py:471
  985.5 10.9 %collective-permute-done.77 = bf16[8,1024]{1,0:T(8,128)(2,1)S(1)} collective-permute-done((bf16[8,1024]{1,0:T(8,128)(2,1)S(1)}, bf16[8,1024]{1,0:T(8,128)(2,1)S(1)}, u32[]{:S(2)}, u32[]{:S(2)}) %collective-permute-start.77) | collective-permute-done | bytes 16416 | tf_op jit(solution)/shard_map/ppermute | solution.py:471
  997.2 8.9 all-gather.3
  (745 shorter events, 488.2 us)
Async XLA Ops:
  70.3 61.0 %all-to-all-start = ((bf16[4,256,1024]{2,1,0:T(8,128)(2,1)}), bf16[4,256,1024]{2,1,0:T(8,128)(2,1)S(1)}, u32[]{:S(2)}, u32[]{:S(2)}) async-start(bf16[4,256,1024]{2,1,0:T(8,128)(2,1)} %get-tuple-element.207), calls=%async_computation | async-start | bytes 4194304 | tf_op jit(solution)/shard_map/all_to_all | solution.py:667
  100.3 45.3 %collective-permute-start.17 = (bf16[128,1024]{1,0:T(8,128)(2,1)}, bf16[128,1024]{1,0:T(8,128)(2,1)}, u32[]{:S(2)}, u32[]{:S(2)}) collective-permute-start(bf16[128,1024]{1,0:T(8,128)(2,1)} %dynamic-slice_bitcast_fusion), channel_id=1, source_target_pairs={{0,1},{1,0},{2,3},{3,2},{4,5},{5,4},{6,7},{7,6},{8,9},{9,8},{10,11... | collective-permute-start | bytes 786440 | tf_op jit(solution)/shard_map/ppermute | solution.py:471
  145.6 52.4 %all-to-all-start.1 = ((bf16[4,256,1024]{2,1,0:T(8,128)(2,1)}), bf16[4,256,1024]{2,1,0:T(8,128)(2,1)}, u32[]{:S(2)}, u32[]{:S(2)}) async-start(bf16[4,256,1024]{2,1,0:T(8,128)(2,1)} %get-tuple-element.223), calls=%async_computation.1 | async-start | bytes 4194304 | tf_op jit(solution)/shard_map/all_to_all | solution.py:667
  152.1 40.3 %collective-permute-start.22 = (bf16[3,128,1024]{2,1,0:T(8,128)(2,1)S(1)}, bf16[3,128,1024]{2,1,0:T(8,128)(2,1)S(1)}, u32[]{:S(2)}, u32[]{:S(2)}) collective-permute-start(bf16[3,128,1024]{2,1,0:T(8,128)(2,1)S(1)} %pad_maximum_fusion.22), channel_id=1, source_target_pairs={{0,4},{4,0},{8,12},{12,8},{16,20},{20,16},{24,28},{28,24},{1,5},{5... | collective-permute-start | bytes 2359304 | tf_op jit(solution)/shard_map/ppermute | solution.py:471
  152.2 40.2 %collective-permute-start.21 = (bf16[3,128,1024]{2,1,0:T(8,128)(2,1)S(1)}, bf16[3,128,1024]{2,1,0:T(8,128)(2,1)S(1)}, u32[]{:S(2)}, u32[]{:S(2)}) collective-permute-start(bf16[3,128,1024]{2,1,0:T(8,128)(2,1)S(1)} %pad_maximum_fusion.22), channel_id=1, source_target_pairs={{0,16},{4,20},{8,24},{12,28},{16,0},{20,4},{24,8},{28,12},{1,17},{... | collective-permute-start | bytes 2359304 | tf_op jit(solution)/shard_map/ppermute | solution.py:471
  152.8 41.4 %collective-permute-start.20 = (bf16[3,128,1024]{2,1,0:T(8,128)(2,1)S(1)}, bf16[3,128,1024]{2,1,0:T(8,128)(2,1)}, u32[]{:S(2)}, u32[]{:S(2)}) collective-permute-start(bf16[3,128,1024]{2,1,0:T(8,128)(2,1)S(1)} %pad_maximum_fusion.22), channel_id=1, source_target_pairs={{0,8},{4,12},{8,0},{12,4},{16,24},{20,28},{24,16},{28,20},{1,9},{5... | collective-permute-start | bytes 2359304 | tf_op jit(solution)/shard_map/ppermute | solution.py:471
  223.7 52.8 %all-to-all-start.2 = ((bf16[4,256,1024]{2,1,0:T(8,128)(2,1)}), bf16[4,256,1024]{2,1,0:T(8,128)(2,1)}, u32[]{:S(2)}, u32[]{:S(2)}) async-start(bf16[4,256,1024]{2,1,0:T(8,128)(2,1)} %get-tuple-element.234), calls=%async_computation.2 | async-start | bytes 4194304 | tf_op jit(solution)/shard_map/all_to_all | solution.py:667
  280.5 69.7 %all-to-all-start.3 = ((bf16[4,256,1024]{2,1,0:T(8,128)(2,1)}), bf16[4,256,1024]{2,1,0:T(8,128)(2,1)}, u32[]{:S(2)}, u32[]{:S(2)}) async-start(bf16[4,256,1024]{2,1,0:T(8,128)(2,1)} %get-tuple-element.266), calls=%async_computation.3 | async-start | bytes 4194304 | tf_op jit(solution)/shard_map/all_to_all | solution.py:667
  301.9 48.4 %collective-permute-start.38 = (bf16[3,128,1024]{2,1,0:T(8,128)(2,1)}, bf16[3,128,1024]{2,1,0:T(8,128)(2,1)}, u32[]{:S(2)}, u32[]{:S(2)}) collective-permute-start(bf16[3,128,1024]{2,1,0:T(8,128)(2,1)} %constant_dynamic-update-slice_fusion.15), channel_id=1, source_target_pairs={{0,4},{4,0},{8,12},{12,8},{16,20},{20,16},{24,28},{28,24},{1,5},{5... | collective-permute-start | bytes 2359304 | tf_op jit(solution)/shard_map/ppermute | solution.py:471
  422.2 108.5 %all-to-all-start.4 = ((bf16[4,2,256,1024]{3,2,1,0:T(8,128)(2,1)}), bf16[4,2,256,1024]{3,2,1,0:T(8,128)(2,1)}, u32[]{:S(2)}, u32[]{:S(2)}) async-start(bf16[4,2,256,1024]{3,2,1,0:T(8,128)(2,1)} %bitcast.447), calls=%async_computation.4 | async-start | bytes 8388608 | tf_op jit(solution)/shard_map/all_to_all | solution.py:667
  427.2 271.8 %all-gather.8.cloned.1.call-start = ((), (), s32[]{:S(2)}) async-start(), calls=%async_computation.7 | async-start | bytes 2359296 | tf_op jit(solution)/shard_map/all_gather | solution.py:622
  433.8 56.7 %collective-permute-start.39 = (bf16[4,4,128,1024]{3,2,1,0:T(8,128)(2,1)}, bf16[4,4,128,1024]{3,2,1,0:T(8,128)(2,1)}, u32[]{:S(2)}, u32[]{:S(2)}) collective-permute-start(bf16[4,4,128,1024]{3,2,1,0:T(8,128)(2,1)} %bitcast.86), channel_id=1, source_target_pairs={{0,4},{4,0},{8,12},{12,8},{16,20},{20,16},{24,28},{28,24},{1,5},{5... | collective-permute-start | bytes 12582920 | tf_op jit(solution)/shard_map/ppermute | solution.py:471
  617.6 76.9 %collective-permute-start.54 = (bf16[3072]{0:T(1024)(128)(2,1)S(1)}, bf16[3072]{0:T(1024)(128)(2,1)S(1)}, u32[]{:S(2)}, u32[]{:S(2)}) collective-permute-start(bf16[3072]{0:T(1024)(128)(2,1)S(1)} %get-tuple-element.515), channel_id=1, source_target_pairs={{0,1},{1,0},{2,3},{3,2},{4,5},{5,4},{6,7},{7,6},{8,9},{9,8},{10,11... | collective-permute-start | bytes 18440 | tf_op jit(solution)/shard_map/ppermute | solution.py:471
  630.8 193.7 %all-gather.10.cloned.1.call-start = ((), (), s32[]{:S(2)}) async-start(), calls=%async_computation.8 | async-start | bytes 2949120 | tf_op jit(solution)/shard_map/all_gather | solution.py:622
  635.1 63.9 %collective-permute-start.49 = (bf16[4,64,1024]{2,1,0:T(8,128)(2,1)S(1)}, bf16[4,64,1024]{2,1,0:T(8,128)(2,1)}, u32[]{:S(2)}, u32[]{:S(2)}) collective-permute-start(bf16[4,64,1024]{2,1,0:T(8,128)(2,1)S(1)} %get-tuple-element.471), channel_id=1, source_target_pairs={{0,16},{4,20},{8,24},{12,28},{16,0},{20,4},{24,8},{28,12},{1,17},{... | collective-permute-start | bytes 1572872 | tf_op jit(solution)/shard_map/ppermute | solution.py:471
  638.4 60.6 %collective-permute-start.50 = (bf16[4,64,1024]{2,1,0:T(8,128)(2,1)S(1)}, bf16[4,64,1024]{2,1,0:T(8,128)(2,1)}, u32[]{:S(2)}, u32[]{:S(2)}) collective-permute-start(bf16[4,64,1024]{2,1,0:T(8,128)(2,1)S(1)} %get-tuple-element.469), channel_id=1, source_target_pairs={{0,8},{4,12},{8,0},{12,4},{16,24},{20,28},{24,16},{28,20},{1,9},{5... | collective-permute-start | bytes 1572872 | tf_op jit(solution)/shard_map/ppermute | solution.py:471
  641.8 57.3 %collective-permute-start.53 = (bf16[2,4,16,1024]{3,2,1,0:T(8,128)(2,1)S(1)}, bf16[2,4,16,1024]{3,2,1,0:T(8,128)(2,1)S(1)}, u32[]{:S(2)}, u32[]{:S(2)}) collective-permute-start(bf16[2,4,16,1024]{3,2,1,0:T(8,128)(2,1)S(1)} %get-tuple-element.467), channel_id=1, source_target_pairs={{0,16},{4,20},{8,24},{12,28},{16,0},{20,4},{24,8},{28,12},{1,17},{... | collective-permute-start | bytes 786440 | tf_op jit(solution)/shard_map/ppermute | solution.py:471
  642.4 56.6 %collective-permute-start.52 = (bf16[2,4,16,1024]{3,2,1,0:T(8,128)(2,1)S(1)}, bf16[2,4,16,1024]{3,2,1,0:T(8,128)(2,1)}, u32[]{:S(2)}, u32[]{:S(2)}) collective-permute-start(bf16[2,4,16,1024]{3,2,1,0:T(8,128)(2,1)S(1)} %slice_bitcast_fusion.40), channel_id=1, source_target_pairs={{0,8},{4,12},{8,0},{12,4},{16,24},{20,28},{24,16},{28,20},{1,9},{5... | collective-permute-start | bytes 786440 | tf_op jit(solution)/shard_map/ppermute | solution.py:471
  767.1 57.3 %all-to-all-start.5 = ((bf16[4,256,1024]{2,1,0:T(8,128)(2,1)}), bf16[4,256,1024]{2,1,0:T(8,128)(2,1)}, u32[]{:S(2)}, u32[]{:S(2)}) async-start(bf16[4,256,1024]{2,1,0:T(8,128)(2,1)} %bitcast.461), calls=%async_computation.5 | async-start | bytes 4194304 | tf_op jit(solution)/shard_map/all_to_all | solution.py:667
  771.8 52.6 %collective-permute-start.65 = (bf16[3072]{0:T(1024)(128)(2,1)S(1)}, bf16[3072]{0:T(1024)(128)(2,1)S(1)}, u32[]{:S(2)}, u32[]{:S(2)}) collective-permute-start(bf16[3072]{0:T(1024)(128)(2,1)S(1)} %add_convert_fusion.29), channel_id=1, source_target_pairs={{0,16},{4,20},{8,24},{12,28},{16,0},{20,4},{24,8},{28,12},{1,17},{... | collective-permute-start | bytes 18440 | tf_op jit(solution)/shard_map/ppermute | solution.py:471
  942.4 73.2 %all-to-all-start.6 = ((bf16[4,256,1024]{2,1,0:T(8,128)(2,1)}), bf16[4,256,1024]{2,1,0:T(8,128)(2,1)}, u32[]{:S(2)}, u32[]{:S(2)}) async-start(bf16[4,256,1024]{2,1,0:T(8,128)(2,1)} %bitcast.460), calls=%async_computation.6 | async-start | bytes 4194304 | tf_op jit(solution)/shard_map/all_to_all | solution.py:667
  946.9 64.3 %all-gather.12.cloned.1.call-start = ((), (), s32[]{:S(2)}) async-start(), calls=%async_computation.9 | async-start | bytes 1769472 | tf_op jit(solution)/shard_map/all_gather | solution.py:622
  952.5 44.0 %collective-permute-start.77 = (bf16[8,1024]{1,0:T(8,128)(2,1)S(1)}, bf16[8,1024]{1,0:T(8,128)(2,1)S(1)}, u32[]{:S(2)}, u32[]{:S(2)}) collective-permute-start(bf16[8,1024]{1,0:T(8,128)(2,1)S(1)} %reshape.567), channel_id=1, source_target_pairs={{0,2},{1,3},{2,0},{3,1},{4,6},{5,7},{6,4},{7,5},{8,10},{9,11},{10,... | collective-permute-start | bytes 49160 | tf_op jit(solution)/shard_map/ppermute | solution.py:471
  952.5 44.0 %collective-permute-start.76 = (bf16[8,1024]{1,0:T(8,128)(2,1)S(1)}, bf16[8,1024]{1,0:T(8,128)(2,1)S(1)}, u32[]{:S(2)}, u32[]{:S(2)}) collective-permute-start(bf16[8,1024]{1,0:T(8,128)(2,1)S(1)} %reshape.567), channel_id=1, source_target_pairs={{0,1},{1,0},{2,3},{3,2},{4,5},{5,4},{6,7},{7,6},{8,9},{9,8},{10,11... | collective-permute-start | bytes 49160 | tf_op jit(solution)/shard_map/ppermute | solution.py:471
  (196 other events, 2785.3 us)
Sparse Core Ops, SparseCore 0:
  630.9 35.4 all-gather.7
  763.1 28.5 all-gather.9
  950.2 25.8 all-gather.11
